TPU v7x, 32 devices: a whole 2x2x4 slice. The times are simulated.
32 devices in a mesh: batch: 16 (over z, y, x), seq: 2 (over core).
Axes of the slice: x: 2, y: 2, z: 4, core: 2. Of those that a mesh axis runs over, the one named last changes fastest.
Arguments:
- tokens: bfloat16 [32768, 768], P(('batch', 'seq')), may hold values from -6 to 6
- seq_lengths: int32 [16, 3], P('batch'), may hold values from 256 to 1024, as said below
- first_gain: float32 [768], replicated, may hold values from 0.5 to 1.5
- first_shift: float32 [768], replicated, may hold values from -2 to 2
- qkv_weight: bfloat16 [768, 2304], replicated, may hold values from -0.21875 to 0.21875
- query_bias: float32 [768], replicated, may hold values from -2 to 2
- value_bias: float32 [768], replicated, may hold values from -2 to 2
- proj_weight: bfloat16 [768, 768], replicated, may hold values from -3.5 to 3.5
- proj_bias: float32 [768], replicated, may hold values from -2 to 2
- second_gain: float32 [768], replicated, may hold values from 0.5 to 1.5
- second_shift: float32 [768], replicated, may hold values from -2 to 2
- expand_weight: bfloat16 [768, 3072], replicated, may hold values from -0.21875 to 0.21875
- expand_bias: float32 [3072], replicated, may hold values from -2 to 2
- shrink_weight: bfloat16 [3072, 768], replicated, may hold values from -0.109375 to 0.109375
- shrink_bias: float32 [768], replicated, may hold values from -2 to 2
- cotangent: bfloat16 [32768, 768], P(('batch', 'seq')), may hold values from -6 to 6
Outputs:
- output: bfloat16 [32768, 768], P(('batch', 'seq'))
- input_grad: float32 [32768, 768], P(('batch', 'seq'))
- grad_first_gain: float32 [768], P(('batch', 'seq'))
- grad_first_shift: float32 [768], P(('batch', 'seq'))
- grad_qkv_weight: float32 [768, 2304], P(('batch', 'seq'))
- grad_query_bias: float32 [768], P(('batch', 'seq'))
- grad_value_bias: float32 [768], P(('batch', 'seq'))
- grad_proj_weight: float32 [768, 768], P(('batch', 'seq'))
- grad_proj_bias: float32 [768], P(('batch', 'seq'))
- grad_second_gain: float32 [768], P(('batch', 'seq'))
- grad_second_shift: float32 [768], P(('batch', 'seq'))
- grad_expand_weight: float32 [768, 3072], P(('batch', 'seq'))
- grad_expand_bias: float32 [3072], P(('batch', 'seq'))
- grad_shrink_weight: float32 [3072, 768], P(('batch', 'seq'))
- grad_shrink_bias: float32 [768], P(('batch', 'seq'))
Inputs may be any that keep to these rules, and one draw needn't show every extreme that they name: `seq_lengths`: row g lists the lengths of the three sequences packed in order into group g; they sum to 2048 and the middle one has exactly 1024 tokens.
All inputs are finite; a program needn't handle non-finite values.
Results may differ from a plain program's by a relative error of at most 0.01.
Values may be sent and summed in bfloat16 or wider, within the bound.
A program may use at most 320 MiB of HBM per device.

v0:
```python
import math

import jax
import jax.numpy as jnp
from jax import lax
from jax.sharding import PartitionSpec as P

H = 12


epsilon = 1e-05
masked_score = -1e30


def layer_norm(v, norm_gain, norm_shift):
    row_mean = jnp.mean(v, axis=-1, keepdims=True)
    centered = v - row_mean
    row_var = jnp.mean(centered * centered, axis=-1, keepdims=True)
    return centered * lax.rsqrt(row_var + epsilon) * norm_gain + norm_shift


def gelu_tanh(v):
    return 0.5 * v * (1.0 + jnp.tanh(0.7978845608028654 * (v + 0.044715 * v * v * v)))


def plain_product(a, b):
    return jnp.dot(a, b, preferred_element_type=jnp.float32)


def left_product(a, b):
    return lax.dot_general(a, b, (((0,), (0,)), ((), ())), preferred_element_type=jnp.float32)


def right_product(a, b):
    return lax.dot_general(a, b, (((1,), (1,)), ((), ())), preferred_element_type=jnp.float32)


def column_sum(a):
    return jnp.sum(a.astype(jnp.float32), axis=0)


def block_scores(query_block, key_block, segment, offset, score_scale):
    block_rows = query_block.shape[0]
    extent = key_block.shape[0]
    raw_scores = (
        jnp.einsum("qhd,khd->hqk", query_block, key_block, preferred_element_type=jnp.float32)
        * score_scale
    )
    query_places = offset + jnp.arange(block_rows, dtype=jnp.int32)
    key_places = jnp.arange(extent, dtype=jnp.int32)
    allowed = (key_places[None, :] <= query_places[:, None]) & (
        segment[offset : offset + block_rows][:, None] == segment[:extent][None, :]
    )
    return jnp.where(allowed[None], raw_scores, masked_score)


def on_device(
    tokens,
    seq_lengths,
    first_gain,
    first_shift,
    qkv_weight,
    query_bias,
    value_bias,
    proj_weight,
    proj_bias,
    second_gain,
    second_shift,
    expand_weight,
    expand_bias,
    shrink_weight,
    shrink_bias,
    cotangent,
):
    local_rows, width = tokens.shape
    shards = lax.axis_size("seq")
    group_rows = local_rows * shards
    local_width = width // shards
    local_heads = H // shards
    head_width = width // H
    score_scale = 1.0 / math.sqrt(head_width)
    block_rows = min(512, group_rows)
    inputs = tokens.astype(jnp.float32)
    normed_first_f, first_pull = jax.vjp(layer_norm, inputs, first_gain, first_shift)
    normed_first = normed_first_f.astype(jnp.bfloat16)
    projected = plain_product(normed_first, qkv_weight)
    queries = (projected[:, :width] + query_bias).astype(jnp.bfloat16)
    key_rows = projected[:, width : 2 * width].astype(jnp.bfloat16)
    values = (projected[:, 2 * width :] + value_bias).astype(jnp.bfloat16)
    packed = jnp.concatenate([queries, key_rows, values], axis=1).reshape(
        local_rows, 3, shards, local_width
    )
    by_heads = lax.all_to_all(packed, "seq", split_axis=2, concat_axis=0, tiled=True)

    def head_view(member):
        return by_heads[:, member, 0, :].reshape(group_rows, local_heads, head_width)

    query_all = head_view(0)
    key_all = head_view(1)
    value_all = head_view(2)
    lengths = seq_lengths[0]
    places = jnp.arange(group_rows, dtype=jnp.int32)
    segment = (places >= lengths[0]).astype(jnp.int32) + (places >= lengths[0] + lengths[1]).astype(
        jnp.int32
    )
    context_list = []
    peak_list = []
    total_list = []
    for offset in range(0, group_rows, block_rows):
        extent = offset + block_rows
        scores = block_scores(
            query_all[offset:extent], key_all[:extent], segment, offset, score_scale
        )
        row_peak = jnp.max(scores, axis=-1, keepdims=True)
        weights = jnp.exp(scores - row_peak)
        row_total = jnp.sum(weights, axis=-1, keepdims=True)
        softmax_rows = (weights / row_total).astype(jnp.bfloat16)
        context_list.append(
            jnp.einsum(
                "hqk,khd->qhd", softmax_rows, value_all[:extent], preferred_element_type=jnp.float32
            )
        )
        peak_list.append(row_peak)
        total_list.append(row_total)
    context_heads = (
        jnp.concatenate(context_list, axis=0).reshape(group_rows, local_width).astype(jnp.bfloat16)
    )
    context_tok = lax.all_to_all(context_heads, "seq", split_axis=0, concat_axis=1, tiled=True)
    attended = plain_product(context_tok, proj_weight) + proj_bias
    middle = inputs + attended
    normed_second_f, second_pull = jax.vjp(layer_norm, middle, second_gain, second_shift)
    normed_second = normed_second_f.astype(jnp.bfloat16)
    expanded = plain_product(normed_second, expand_weight) + expand_bias
    activated_f, gelu_pull = jax.vjp(gelu_tanh, expanded)
    activated = activated_f.astype(jnp.bfloat16)
    shrunk = plain_product(activated, shrink_weight) + shrink_bias
    output = (middle + shrunk).astype(jnp.bfloat16)
    grad_shrink_weight = left_product(activated, cotangent)
    grad_shrink_bias = column_sum(cotangent)
    grad_activated = right_product(cotangent, shrink_weight)
    (grad_expanded_f,) = gelu_pull(grad_activated)
    grad_expanded = grad_expanded_f.astype(jnp.bfloat16)
    grad_expand_weight = left_product(normed_second, grad_expanded)
    grad_expand_bias = column_sum(grad_expanded)
    grad_normed_second = right_product(grad_expanded, expand_weight)
    back_middle, grad_second_gain, grad_second_shift = second_pull(grad_normed_second)
    grad_middle = cotangent.astype(jnp.float32) + back_middle
    grad_attended = grad_middle.astype(jnp.bfloat16)
    grad_proj_weight = left_product(context_tok, grad_attended)
    grad_proj_bias = column_sum(grad_attended)
    grad_context = right_product(grad_attended, proj_weight).astype(jnp.bfloat16)
    grad_context_heads = lax.all_to_all(
        grad_context, "seq", split_axis=1, concat_axis=0, tiled=True
    ).reshape(group_rows, local_heads, head_width)
    query_grads = []
    grad_keys = jnp.zeros((group_rows, local_heads, head_width), jnp.float32)
    grad_values = jnp.zeros((group_rows, local_heads, head_width), jnp.float32)
    for position, offset in enumerate(range(0, group_rows, block_rows)):
        extent = offset + block_rows
        query_block = query_all[offset:extent]
        scores = block_scores(query_block, key_all[:extent], segment, offset, score_scale)
        softmax_f = jnp.exp(scores - peak_list[position]) / total_list[position]
        grad_block = grad_context_heads[offset:extent]
        grad_weights = jnp.einsum(
            "qhd,khd->hqk", grad_block, value_all[:extent], preferred_element_type=jnp.float32
        )
        row_inner = jnp.sum(softmax_f * grad_weights, axis=-1, keepdims=True)
        grad_scores = (softmax_f * (grad_weights - row_inner)).astype(jnp.bfloat16)
        query_grads.append(
            jnp.einsum(
                "hqk,khd->qhd", grad_scores, key_all[:extent], preferred_element_type=jnp.float32
            )
            * score_scale
        )
        grad_keys = grad_keys.at[:extent].add(
            jnp.einsum("hqk,qhd->khd", grad_scores, query_block, preferred_element_type=jnp.float32)
            * score_scale
        )
        grad_values = grad_values.at[:extent].add(
            jnp.einsum(
                "hqk,qhd->khd",
                softmax_f.astype(jnp.bfloat16),
                grad_block,
                preferred_element_type=jnp.float32,
            )
        )
    grad_queries = jnp.concatenate(query_grads, axis=0).reshape(group_rows, local_width)
    stacked = jnp.stack(
        [
            grad_queries,
            grad_keys.reshape(group_rows, local_width),
            grad_values.reshape(group_rows, local_width),
        ],
        axis=1,
    )
    stacked = stacked.astype(jnp.bfloat16).reshape(group_rows, 3, 1, local_width)
    back_rows = lax.all_to_all(stacked, "seq", split_axis=0, concat_axis=2, tiled=True).reshape(
        local_rows, 3 * width
    )
    grad_qkv_weight = left_product(normed_first, back_rows)
    grad_query_bias = column_sum(back_rows[:, :width])
    grad_value_bias = column_sum(back_rows[:, 2 * width :])
    grad_normed_first = right_product(back_rows, qkv_weight)
    back_inputs, grad_first_gain, grad_first_shift = first_pull(grad_normed_first)
    input_grad = grad_middle + back_inputs
    summed = (
        lax.psum_scatter(grad_first_gain, ("batch", "seq"), scatter_dimension=0, tiled=True),
        lax.psum_scatter(grad_first_shift, ("batch", "seq"), scatter_dimension=0, tiled=True),
        lax.psum_scatter(grad_qkv_weight, ("batch", "seq"), scatter_dimension=0, tiled=True),
        lax.psum_scatter(grad_query_bias, ("batch", "seq"), scatter_dimension=0, tiled=True),
        lax.psum_scatter(grad_value_bias, ("batch", "seq"), scatter_dimension=0, tiled=True),
        lax.psum_scatter(grad_proj_weight, ("batch", "seq"), scatter_dimension=0, tiled=True),
        lax.psum_scatter(grad_proj_bias, ("batch", "seq"), scatter_dimension=0, tiled=True),
        lax.psum_scatter(grad_second_gain, ("batch", "seq"), scatter_dimension=0, tiled=True),
        lax.psum_scatter(grad_second_shift, ("batch", "seq"), scatter_dimension=0, tiled=True),
        lax.psum_scatter(grad_expand_weight, ("batch", "seq"), scatter_dimension=0, tiled=True),
        lax.psum_scatter(grad_expand_bias, ("batch", "seq"), scatter_dimension=0, tiled=True),
        lax.psum_scatter(grad_shrink_weight, ("batch", "seq"), scatter_dimension=0, tiled=True),
        lax.psum_scatter(grad_shrink_bias, ("batch", "seq"), scatter_dimension=0, tiled=True),
    )
    return (
        output,
        input_grad,
        summed[0],
        summed[1],
        summed[2],
        summed[3],
        summed[4],
        summed[5],
        summed[6],
        summed[7],
        summed[8],
        summed[9],
        summed[10],
        summed[11],
        summed[12],
    )


def solution(mesh):
    in_specs = (
        P(("batch", "seq"), None),
        P("batch", None),
        P(),
        P(),
        P(),
        P(),
        P(),
        P(),
        P(),
        P(),
        P(),
        P(),
        P(),
        P(),
        P(),
        P(("batch", "seq"), None),
    )
    out_specs = (
        P(("batch", "seq"), None),
        P(("batch", "seq"), None),
        P(("batch", "seq")),
        P(("batch", "seq")),
        P(("batch", "seq"), None),
        P(("batch", "seq")),
        P(("batch", "seq")),
        P(("batch", "seq"), None),
        P(("batch", "seq")),
        P(("batch", "seq")),
        P(("batch", "seq")),
        P(("batch", "seq"), None),
        P(("batch", "seq")),
        P(("batch", "seq"), None),
        P(("batch", "seq")),
    )
    return jax.shard_map(
        on_device, mesh=mesh, in_specs=in_specs, out_specs=out_specs, check_vma=False
    )
```

profile of v0, /device:TPU:0, one launch (start us, length us, event | category | flops | bytes accessed | tf_op | source)
XLA Modules:
  0.0 893.9 jit_solution(11788675774933450498)
XLA Ops:
  22.2 9.9 %reshape.631 = bf16[1024,3,2,384]{3,2,1,0:T(2,128)(2,1)} reshape(bf16[1024,2304]{1,0:T(8,128)(2,1)} %pad_maximum_fusion.1) | data formatting | bytes 9437184 | tf_op jit(solution)/shard_map/reshape | solution.py:90
  102.2 10.2 %fusion.164 = (f32[6,512]{1,0:T(8,128)S(1)}, f32[6,512,1024]{2,1,0:T(8,128)}) fusion(pred[512,1024]{1,0:T(8,128)(4,1)} %fusion.71, bf16[512,6,64]{0,2,1:T(8,128)(2,1)} %bitcast.163, bf16[1024,6,64]{0,2,1:T(8,128)(2,1)} %bitcast.161), kind=kOutput, calls=%fused_computation.207 | convolution fusion | flops 415237120 | bytes 14299136 | tf_op jit(solution)/shard_map/sub | solution.py:115
  112.4 7.7 fusion.101
  120.1 20.8 %fusion.163 = (f32[6,512]{1,0:T(8,128)S(1)}, f32[6,512,1536]{2,1,0:T(8,128)}) fusion(pred[512,1536]{1,0:T(8,128)(4,1)} %fusion.53, bf16[512,6,64]{0,2,1:T(8,128)(2,1)} %bitcast.175, bf16[1536,6,64]{0,2,1:T(8,128)(2,1)} %bitcast.159), kind=kOutput, calls=%fused_computation.206 | convolution fusion | flops 622855680 | bytes 21245952 | tf_op jit(solution)/shard_map/sub | solution.py:115
  140.9 10.5 %fusion.114 = bf16[512,6,64]{0,2,1:T(8,128)(2,1)} fusion(bf16[1536,6,64]{0,2,1:T(8,128)(2,1)} %bitcast.177, f32[6,512,1536]{2,1,0:T(8,128)} %get-tuple-element.231, f32[6,512]{1,0:T(8,128)S(1)} %get-tuple-element.230), kind=kOutput, calls=%fused_computation.150 | convolution fusion | flops 613613568 | bytes 20459520 | tf_op jit(solution)/shard_map/hqk,khd->qhd/dot_general | solution.py:119
  151.4 14.7 %fusion.162 = (f32[6,512]{1,0:T(8,128)S(1)}, f32[6,512,2048]{2,1,0:T(8,128)}) fusion(pred[512,2048]{1,0:T(8,128)(4,1)} %fusion.35, bf16[512,6,64]{0,2,1:T(8,128)(2,1)} %bitcast.173, bf16[2048,6,64]{0,2,1:T(8,128)(2,1)} %bitcast.152), kind=kOutput, calls=%fused_computation.205 | convolution fusion | flops 830474240 | bytes 28192768 | tf_op jit(solution)/shard_map/sub | solution.py:115
  166.2 10.9 %fusion.111 = bf16[512,6,64]{0,2,1:T(8,128)(2,1)S(1)} fusion(bf16[2048,6,64]{0,2,1:T(8,128)(2,1)} %bitcast.165, f32[6,512,2048]{2,1,0:T(8,128)} %get-tuple-element.229, f32[6,512]{1,0:T(8,128)S(1)} %get-tuple-element.228), kind=kOutput, calls=%fused_computation.149 | convolution fusion | flops 818085888 | bytes 27144192 | tf_op jit(solution)/shard_map/hqk,khd->qhd/dot_general | solution.py:119
  204.3 19.1 %convert_reduce_fusion = (f32[3072]{0:T(1024)}, bf16[1024,3072]{1,0:T(8,128)(2,1)}) fusion(bf16[1024,768]{1,0:T(8,128)(2,1)S(1)} %copy-done.20, bf16[3072,768]{1,0:T(8,128)(2,1)} %param.49, f32[1024,3072]{1,0:T(8,128)S(1)} %fusion.152, f32[3072]{0:T(1024)S(1)} %copy-done.73), kind=kOutput, calls=%fused_computation.24 | convolution fusion | flops 4916769792 | bytes 25190400 | tf_op jit(solution)/shard_map/dot_general | solution.py:35
  223.4 10.7 %fusion.168 = (f32[768]{0:T(1024)}, f32[1024,768]{1,0:T(8,128)}) fusion(bf16[1024,3072]{1,0:T(8,128)(2,1)} %get-tuple-element.251, bf16[768,3072]{1,0:T(8,128)(2,1)} %param.47), kind=kOutput, calls=%fused_computation.211 | convolution fusion | flops 4832623616 | bytes 14158848 | tf_op jit(solution)/shard_map/dot_general | solution.py:35
  270.5 7.5 multiply_reduce_fusion.3
  284.6 13.0 %multiply_reduce_fusion.1 = (f32[6,512]{1,0:T(8,128)}, f32[6,512,1536]{2,1,0:T(8,128)}) fusion(f32[6,512,1536]{2,1,0:T(8,128)} %get-tuple-element.231, f32[6,512]{1,0:T(8,128)S(1)} %copy-done.55, bf16[1536,6,64]{0,2,1:T(8,128)(2,1)S(1)} %bitcast.178, bf16[2048,6,64]{0,2,1:T(8,128)(2,1)S(1)} %copy-done.21), kind=kOutput, calls=%fused_computation.12 | convolution fusion | flops 618132480 | bytes 39350272 | tf_op jit(solution)/shard_map/qhd,khd->hqk/dot_general | solution.py:164
  297.6 17.8 %multiply_reduce_fusion = (f32[6,512]{1,0:T(8,128)}, f32[6,512,2048]{2,1,0:T(8,128)}) fusion(f32[6,512,2048]{2,1,0:T(8,128)} %get-tuple-element.229, f32[6,512]{1,0:T(8,128)} %copy-done.57, bf16[2048,6,64]{0,2,1:T(8,128)(2,1)} %bitcast.166, bf16[2048,6,64]{0,2,1:T(8,128)(2,1)} %reshape.632), kind=kOutput, calls=%fused_computation.5 | convolution fusion | flops 824177664 | bytes 52326400 | tf_op jit(solution)/shard_map/qhd,khd->hqk/dot_general | solution.py:164
  322.5 7.6 fusion.66
  330.1 11.3 %fusion.45 = bf16[2048,6,64]{0,2,1:T(8,128)(2,1)} fusion(f32[2048,6,64]{0,2,1:T(8,128)S(1)} %fusion.66, bf16[2048,6,64]{0,2,1:T(8,128)(2,1)S(1)} %copy-done.22, f32[6,512,2048]{2,1,0:T(8,128)} %get-tuple-element.229, f32[6,512]{1,0:T(8,128)S(1)} %copy-done.58), kind=kOutput, calls=%fused_computation.84 | convolution fusion | flops 819462144 | bytes 30294016 | tf_op jit(solution)/shard_map/hqk,qhd->khd/dot_general | solution.py:180
  341.4 8.9 copy.131
  358.4 9.2 %multiply_convert_fusion.2 = bf16[6,512,1024]{2,1,0:T(8,128)(2,1)S(1)} fusion(f32[6,512,1024]{2,1,0:T(8,128)} %get-tuple-element.241, f32[6,512]{1,0:T(8,128)S(1)} %copy-done.65, f32[6,512,1024]{2,1,0:T(8,128)} %get-tuple-element.233, f32[6,512]{1,0:T(8,128)S(1)} %copy-done.63), kind=kLoop, calls=%fused_computation.25 | loop fusion | flops 12582912 | bytes 31481856 | tf_op jit(solution)/shard_map/convert_element_type | solution.py:168
  371.8 12.7 %multiply_convert_fusion.1 = bf16[6,512,1536]{2,1,0:T(8,128)(2,1)S(1)} fusion(f32[6,512,1536]{2,1,0:T(8,128)} %get-tuple-element.243, f32[6,512]{1,0:T(8,128)S(1)} %copy-done.56, f32[6,512,1536]{2,1,0:T(8,128)} %get-tuple-element.231, f32[6,512]{1,0:T(8,128)S(1)} %copy-done.55), kind=kLoop, calls=%fused_computation.11 | loop fusion | flops 18874368 | bytes 47210496 | tf_op jit(solution)/shard_map/convert_element_type | solution.py:168
  390.1 16.3 %multiply_convert_fusion = bf16[6,512,2048]{2,1,0:T(8,128)(2,1)S(1)} fusion(f32[6,512,2048]{2,1,0:T(8,128)} %get-tuple-element.245, f32[6,512]{1,0:T(8,128)S(1)} %copy-done.64, f32[6,512,2048]{2,1,0:T(8,128)} %get-tuple-element.229, f32[6,512]{1,0:T(8,128)S(1)} %copy-done.59), kind=kLoop, calls=%fused_computation.4 | loop fusion | flops 25165824 | bytes 62939136 | tf_op jit(solution)/shard_map/convert_element_type | solution.py:168
  411.5 8.6 copy.130
  422.9 8.6 fusion.108
  432.8 8.4 copy.129
  441.3 12.0 %pad_maximum_fusion = bf16[2048,3,1,384]{3,1,2,0:T(4,128)(2,1)S(1)} fusion(bf16[2048,1,1,384]{3,1,2,0:T(2,128)(2,1)} %copy.131, bf16[2048,1,1,384]{3,1,2,0:T(2,128)(2,1)} %copy.130, bf16[2048,1,1,384]{3,1,2,0:T(2,128)(2,1)} %copy.129), kind=kLoop, calls=%fused_computation.39 | loop fusion | flops 14155776 | bytes 9437184 | tf_op jit(solution)/shard_map/stack | solution.py:188
  453.3 8.8 all_to_all.66
  465.0 6.7 copy.133
  471.7 9.9 %fusion.147 = f32[768,2304]{1,0:T(8,128)} fusion(bf16[1024,2304]{0,1:T(8,128)(2,1)} %bitcast.147, bf16[1024,768]{0,1:T(8,128)(2,1)} %copy.105, f32[768]{0:T(1024)S(1)} %copy-done.78, f32[768]{0:T(1024)S(1)} %copy-done.50, f32[1024]{0:T(1024)S(1)} %copy-done.45, f32[1024]{0:T(1024)S(1)} %copy-done.42), kind=kOutput, calls=%fused_computation.193 | convolution fusion | flops 3628597248 | bytes 13383680 | tf_op jit(solution)/shard_map/dot_general | solution.py:31
  482.3 13.3 %fusion.153 = f32[3072,768]{1,0:T(8,128)} fusion(bf16[1024,768]{1,0:T(8,128)(2,1)} %param.51, f32[1024,3072]{1,0:T(8,128)} %copy-done.13, f32[3072]{0:T(1024)S(1)} %copy-done.74), kind=kOutput, calls=%fused_computation.197 | convolution fusion | flops 4863295488 | bytes 23605248 | tf_op jit(solution)/shard_map/dot_general | solution.py:31
  496.3 11.1 %fusion.151 = f32[768,3072]{1,0:T(8,128)} fusion(bf16[1024,3072]{1,0:T(8,128)(2,1)} %get-tuple-element.251, f32[1024,768]{0,1:T(8,128)} %copy-done.4, f32[768]{0:T(1024)S(1)} %copy-done.40, f32[768]{0:T(1024)S(1)} %copy-done.34, f32[1024]{0:T(1024)S(1)} %copy-done.32, f32[1024]{0:T(1024)S(1)} %copy-done.30), kind=kOutput, calls=%fused_computation.195 | convolution fusion | flops 4835770368 | bytes 18888704 | tf_op jit(solution)/shard_map/dot_general | solution.py:31
  508.1 12.4 %add_convert_fusion = bf16[1024,768]{0,1:T(8,128)(2,1)} fusion(f32[1024,768]{0,1:T(8,128)} %copy-done.4, bf16[3072,768]{1,0:T(8,128)(2,1)} %param.49, f32[768]{0:T(1024)S(1)} %copy-done.79, f32[1024,3072]{1,0:T(8,128)} %copy-done.13, f32[3072]{0:T(1024)S(1)} %copy-done.75), kind=kOutput, calls=%fused_computation.93 | convolution fusion | flops 4865654784 | bytes 22035456 | tf_op jit(solution)/shard_map/dot_general | solution.py:27
  523.1 8.6 fusion.167
  548.0 43.8 %all-reduce.11 = (f32[768]{0:T(1024)}, f32[768]{0:T(1024)}, f32[768]{0:T(1024)}, f32[768]{0:T(1024)}, f32[768]{0:T(1024)}, /*index=5*/f32[768]{0:T(1024)}, f32[768]{0:T(1024)S(1)}, f32[3072]{0:T(1024)}, f32[768]{0:T(1024)S(1)}) all-reduce(f32[768]{0:T(1024)} %get-tuple-element.189, ...), channel_id=2, replica_groups=mesh['batch'=16,'seq'=2] {'batch','seq'}, use_global_device_ids=true, to_apply=%region_21.22.clone | all-reduce | flops 9216 | bytes 73728
  605.4 139.5 %reduce-scatter.11.cloned.1.call-done = f32[96,768]{1,0:T(8,128)} async-done(((f32[3072,768]{1,0:T(8,128)}), f32[96,768]{1,0:T(8,128)}) %reduce-scatter.11.cloned.1.call-update) | async-done | bytes 294928 | tf_op jit(solution)/shard_map/reduce_scatter | solution.py:218
  744.9 142.0 %reduce-scatter.9.cloned.1.call-done = f32[24,3072]{1,0:T(8,128)} async-done(((f32[768,3072]{1,0:T(8,128)}), f32[24,3072]{1,0:T(8,128)}) %reduce-scatter.9.cloned.1.call-update) | async-done | bytes 294928 | tf_op jit(solution)/shard_map/reduce_scatter | solution.py:216
  (278 shorter events, 225.1 us)
Async XLA Ops:
  7.2 7.1 copy-start
  7.2 7.1 copy-start.49
  7.2 7.0 copy-start.77
  37.2 7.3 copy-start.72
  37.2 11.0 %all-to-all-start = ((bf16[1024,3,2,384]{3,0,1,2:T(8,128)(2,1)}), bf16[1024,3,2,384]{3,0,1,2:T(8,128)(2,1)}, u32[]{:S(2)}, u32[]{:S(2)}) async-start(bf16[1024,3,2,384]{3,0,1,2:T(8,128)(2,1)} %copy.106), calls=%async_computation | async-start | bytes 9437184 | tf_op jit(solution)/shard_map/all_to_all | solution.py:93
  79.7 9.6 %copy-start.69 = (s32[512]{0:T(512)S(1)}, s32[512]{0:T(512)}, u32[]{:S(2)}) copy-start(s32[512]{0:T(512)} %get-tuple-element.224) | copy-start | bytes 6148
  112.4 7.7 copy-start.60
  140.9 10.5 %copy-start.54 = (f32[6,512]{1,0:T(8,128)}, f32[6,512]{1,0:T(8,128)S(1)}, u32[]{:S(2)}) copy-start(f32[6,512]{1,0:T(8,128)S(1)} %get-tuple-element.230) | copy-start | bytes 36868
  166.1 10.9 %copy-start.57 = (f32[6,512]{1,0:T(8,128)}, f32[6,512]{1,0:T(8,128)S(1)}, u32[]{:S(2)}) copy-start(f32[6,512]{1,0:T(8,128)S(1)} %get-tuple-element.228) | copy-start | bytes 36868
  166.1 10.9 %copy-start.35 = (bf16[512,6,64]{0,2,1:T(8,128)(2,1)S(1)}, bf16[512,6,64]{0,2,1:T(8,128)(2,1)}, u32[]{:S(2)}) copy-start(bf16[512,6,64]{0,2,1:T(8,128)(2,1)} %fusion.105) | copy-start | bytes 1179652
  166.2 10.9 %copy-start.36 = (bf16[512,6,64]{0,2,1:T(8,128)(2,1)S(1)}, bf16[512,6,64]{0,2,1:T(8,128)(2,1)}, u32[]{:S(2)}) copy-start(bf16[512,6,64]{0,2,1:T(8,128)(2,1)} %fusion.101) | copy-start | bytes 1179652
  166.2 10.9 %copy-start.37 = (bf16[512,6,64]{0,2,1:T(8,128)(2,1)S(1)}, bf16[512,6,64]{0,2,1:T(8,128)(2,1)}, u32[]{:S(2)}) copy-start(bf16[512,6,64]{0,2,1:T(8,128)(2,1)} %fusion.114) | copy-start | bytes 1179652
  185.3 7.6 copy-start.76
  185.3 7.6 all-to-all-start.1
  190.0 415.3 %reduce-scatter.7.cloned.1.call-start = ((), (), s32[]{:S(2)}) async-start(), calls=%async_computation.9 | async-start | bytes 2433024 | tf_op jit(solution)/shard_map/reduce_scatter | solution.py:212
  197.0 45.1 %copy-start.29 = (f32[1024]{0:T(1024)}, f32[1024]{0:T(1024)S(1)}, u32[]{:S(2)}) copy-start(f32[1024]{0:T(1024)S(1)} %broadcast_multiply_fusion) | copy-start | bytes 12292
  198.7 43.5 %copy-start.31 = (f32[1024]{0:T(1024)}, f32[1024]{0:T(1024)S(1)}, u32[]{:S(2)}) copy-start(f32[1024]{0:T(1024)S(1)} %fusion.134) | copy-start | bytes 12292
  204.3 19.1 %copy-start.13 = (f32[1024,3072]{1,0:T(8,128)}, f32[1024,3072]{1,0:T(8,128)S(1)}, u32[]{:S(2)}) copy-start(f32[1024,3072]{1,0:T(8,128)S(1)} %fusion.152) | copy-start | bytes 37748740
  250.3 355.0 %reduce-scatter.5.cloned.1.call-start = ((), (), s32[]{:S(2)}) async-start(), calls=%async_computation.8 | async-start | bytes 7299072 | tf_op jit(solution)/shard_map/reduce_scatter | solution.py:209
  265.3 12.6 %slice-start = ((s8[12582912]{0:T(1024)(128)(4,1)}), s8[4194304]{0:T(1024)(128)(4,1)S(1)}, s32[]{:S(2)}) async-start(s8[12582912]{0:T(1024)(128)(4,1)} %bitcast.150), calls=%async_computation.12 | async-start | bytes 8388608
  265.4 12.6 %slice-start.1 = ((s8[12582912]{0:T(1024)(128)(4,1)}), s8[4194304]{0:T(1024)(128)(4,1)S(1)}, s32[]{:S(2)}) async-start(s8[12582912]{0:T(1024)(128)(4,1)} %bitcast.150), calls=%async_computation.13 | async-start | bytes 8388608
  270.5 7.5 slice-start.2
  270.5 7.5 copy-start.28
  270.5 7.5 copy-start.61
  322.5 7.6 copy-start.58
  358.4 9.2 %copy-start.16 = (bf16[1024,1,1,384]{0,3,2,1:T(8,128)(2,1)S(1)}, bf16[1024,1,1,384]{0,3,2,1:T(8,128)(2,1)}, u32[]{:S(2)}) copy-start(bf16[1024,1,1,384]{0,3,2,1:T(8,128)(2,1)} %copy.114) | copy-start | bytes 2359300
  371.8 12.8 %copy-start.15 = (bf16[1536,1,1,384]{0,3,2,1:T(8,128)(2,1)S(1)}, bf16[1536,1,1,384]{0,3,2,1:T(8,128)(2,1)}, u32[]{:S(2)}) copy-start(bf16[1536,1,1,384]{0,3,2,1:T(8,128)(2,1)} %copy.117) | copy-start | bytes 3538948
  390.1 16.4 %copy-start.25 = (bf16[512,1,1,384]{0,3,2,1:T(8,128)(2,1)S(1)}, bf16[512,1,1,384]{0,3,2,1:T(8,128)(2,1)}, u32[]{:S(2)}) copy-start(bf16[512,1,1,384]{0,3,2,1:T(8,128)(2,1)} %copy.119) | copy-start | bytes 1179652
  422.8 8.6 copy-start.18
  422.9 8.6 copy-start.19
  481.6 263.3 %reduce-scatter.11.cloned.1.call-start = ((), (), s32[]{:S(2)}) async-start(), calls=%async_computation.11 | async-start | bytes 9732096 | tf_op jit(solution)/shard_map/reduce_scatter | solution.py:218
  495.7 391.2 %reduce-scatter.9.cloned.1.call-start = ((), (), s32[]{:S(2)}) async-start(), calls=%async_computation.10 | async-start | bytes 9732096 | tf_op jit(solution)/shard_map/reduce_scatter | solution.py:216
  (59 other events, 201.8 us)
Sparse Core Ops, SparseCore 0:
  250.5 101.8 reduce-scatter.6
  481.7 121.7 reduce-scatter.4
  610.0 134.8 reduce-scatter.10
  752.2 134.6 reduce-scatter.8
where the time goes:
time: 903 us; the launch traced here: 894 us
  matrix products  292 us (32%)
  waiting for transfers between devices  282 us (31%)
  local copies, waits for them, and re-layouts  140 us (16%)
  other arithmetic  94.7 us (10%)
  blocking collectives  57.7 us (6%)
  between operations  16.5 us (2%)
  starting transfers between devices  11.1 us (1%)
    reduce_scatter x1, waiting for transfers between devices, on_device(): lax.psum_scatter(grad_expand_weight, ('batch', 'seq'), scatter_dimension=...  142 us
    reduce_scatter x1, waiting for transfers between devices, on_device(): lax.psum_scatter(grad_shrink_weight, ('batch', 'seq'), scatter_dimension=...  139 us
    sub x4, matrix products, on_device(): weights = jnp.exp(scores - row_peak)  51.9 us
    dot_general x4, matrix products, on_device(): jnp.einsum('qhd,khd->hqk', grad_block, value_all[:extent], preferred_elem...  44.8 us
    convert_element_type x4, other arithmetic, on_device(): grad_scores = (softmax_f * (grad_weights - row_inner)).astype(jnp.bfloat16)  44.7 us
    unnamed x1, blocking collectives  43.8 us
    dot_general x4, matrix products, right_product(): lax.dot_general(a, b, (((1,), (1,)), ((), ())), preferred_element_type=jn...  41.6 us
    dot_general x4, matrix products, left_product(): lax.dot_general(a, b, (((0,), (0,)), ((), ())), preferred_element_type=jn...  38.6 us
  transfers between devices with their start and end apart: 6, of which 3 were waited for; matrix products, arithmetic and copies ran while one was open for 33% of the time, Pallas kernels for 0%

commit v1 on v0

v1 whole, which is shorter than its diff:
```python
import functools
import math

import jax
import jax.numpy as jnp
from jax import lax
from jax.experimental import pallas as pl
from jax.experimental.pallas import tpu as pltpu
from jax.sharding import PartitionSpec as P

f32 = jnp.float32
bf16 = jnp.bfloat16
MESH = pl.DeviceIdType.MESH
ANY = pl.BlockSpec(memory_space=pl.ANY)
VMEM = pl.BlockSpec(memory_space=pltpu.VMEM)
SMEM = pl.BlockSpec(memory_space=pltpu.SMEM)

H = 12
epsilon = 1e-05
masked_score = -1e30
ROWS = 1024
SWAP = 768
D = 768
FF = 3072
PAIRS = 6
BLK = 256
DEST = 32
VMEM_LIMIT = 63 * 2**20
GELU_C = 0.7978845608028654


def nn(a, b):
    return lax.dot_general(a, b, (((1,), (0,)), ((), ())), preferred_element_type=f32)


def nt(a, b):
    return lax.dot_general(a, b, (((1,), (1,)), ((), ())), preferred_element_type=f32)


def row_stats(v):
    mean = jnp.mean(v, axis=-1, keepdims=True)
    centered = v - mean
    var = jnp.mean(centered * centered, axis=-1, keepdims=True)
    return centered * lax.rsqrt(var + epsilon), lax.rsqrt(var + epsilon)


def lane_ids(shape):
    return lax.broadcasted_iota(jnp.int32, shape, 1)


def row_ids(shape):
    return lax.broadcasted_iota(jnp.int32, shape, 0)


def split3(v):
    hi = v.astype(bf16).astype(f32)
    rest = v - hi
    mid = rest.astype(bf16).astype(f32)
    return hi, mid, rest - mid


def rotated(m, shift, i):
    coarse = lax.shift_right_logical(shift, 8)
    fine = lax.bitwise_and(shift, 255)

    def two(k):
        blocks = [m[pl.ds(pl.multiple_of(((i + k + n) % 4) * BLK, BLK), BLK), :] for n in range(2)]
        return jnp.concatenate(blocks, axis=0)

    part = jnp.where(coarse == 1, two(1), jnp.where(coarse == 2, two(2), two(3)))
    shape = (BLK, 2 * BLK)
    pick = (lane_ids(shape) == row_ids(shape) + fine).astype(f32).astype(bf16)
    return nn(pick, part)


def forward_kernel(
    lens, tok_h, cot_h, gain1, shift1, wq_h, qb, vb, wp_h, pb, gain2, shift2,
    x_h, cotr_h, n1_h, qx_h, kx_h, v_h, ctx_h, mid_h, n2_h,
    tok, cot, tok_in, cot_in, dbl, x, cotr, n1, qx, kx, v, ctx, mid, n2, wq, wp,
    load_sem, send_sem, recv_sem, out_sem,
):
    b = lax.axis_index("batch")
    c = lax.axis_index("seq")
    partner = (b, 1 - c)
    a = lens[0, 0]
    loads = [
        pltpu.make_async_copy(src, dst, load_sem.at[i])
        for i, (src, dst) in enumerate(((tok_h, tok), (wq_h, wq), (cot_h, cot), (wp_h, wp)))
    ]
    for cp in loads:
        cp.start()
    barrier = pltpu.get_barrier_semaphore()
    pl.semaphore_signal(barrier, inc=1, device_id=partner, device_id_type=MESH)
    pl.semaphore_wait(barrier, 1)
    swaps = [
        pltpu.make_async_remote_copy(
            src_ref=src.at[pl.ds(0, SWAP)], dst_ref=dst, send_sem=send_sem.at[i],
            recv_sem=recv_sem.at[i], device_id=partner, device_id_type=MESH)
        for i, (src, dst) in enumerate(((tok_h, tok_in), (cot_h, cot_in)))
    ]
    for cp in swaps:
        cp.start()

    def merged(own, other, r):
        m = own[pl.ds(r, BLK), :].astype(f32)
        o = other[pl.ds(r, BLK), :].astype(f32)
        return jnp.where(row_ids((BLK, D)) + r >= a, m, o)

    def fill(own, other):
        def step(i, _):
            r = pl.multiple_of(i * BLK, BLK)
            dbl[pl.ds(r, BLK), :] = merged(own, other, r).astype(bf16)
            return 0
        lax.fori_loop(0, SWAP // BLK, step, 0)
        dbl[SWAP:ROWS, :] = own[SWAP:ROWS, :]

    loads[0].wait()
    swaps[0].wait()
    fill(tok, tok_in)
    loads[1].wait()

    lane = lane_ids((BLK, 128))
    bound = jnp.where(c == 0, 0, ROWS - a)

    def project(i, _):
        r = pl.multiple_of(i * BLK, BLK)
        rows = pl.ds(r, BLK)
        xt = rotated(dbl, a, i)
        x[rows, :] = xt.astype(bf16)
        normed, _unused = row_stats(xt)
        nt_ = (normed * gain1[...].reshape(1, D) + shift1[...].reshape(1, D)).astype(bf16)
        n1[rows, :] = nt_
        late = row_ids((BLK, 128)) + r >= bound
        q_flag = jnp.where(late, 1.0, 0.0).astype(f32)
        k_flag = jnp.where(late, 0.0, masked_score).astype(f32)
        q = nn(nt_, wq[:, 0:D]) + qb[...].reshape(1, D)
        q = q.astype(bf16).astype(f32) * 0.125
        k = nn(nt_, wq[:, D : 2 * D])
        vv = nn(nt_, wq[:, 2 * D : 3 * D]) + vb[...].reshape(1, D)
        v[rows, :] = vv.astype(bf16)
        for p in range(PAIRS):
            qp = q[:, 128 * p : 128 * p + 128]
            kp = k[:, 128 * p : 128 * p + 128]
            for s in range(2):
                mine = lane < 64 if s == 0 else lane >= 64
                base = 64 if s == 0 else 0
                q_aug = jnp.where(lane == base, q_flag, 0.0)
                k_aug = jnp.where(lane == base, k_flag, 1.0)
                k_aug = jnp.where(lane > base + 3, 0.0, k_aug)
                at = 256 * p + 128 * s
                qx[rows, at : at + 128] = jnp.where(mine, qp, q_aug).astype(bf16)
                kx[rows, at : at + 128] = jnp.where(mine, kp, k_aug).astype(bf16)
        return 0

    lax.fori_loop(0, ROWS // BLK, project, 0)
    early = [
        pltpu.make_async_copy(src, dst, out_sem.at[i])
        for i, (src, dst) in enumerate(((x, x_h), (n1, n1_h), (kx, kx_h), (v, v_h)))
    ]
    for cp in early:
        cp.start()

    causal = lane_ids((BLK, BLK)) <= row_ids((BLK, BLK))

    def attend(p, _):
        at = pl.multiple_of(p * 256, 256)
        vat = pl.multiple_of(p * 128, 128)
        for i in range(ROWS // BLK):
            rows = slice(BLK * i, BLK * i + BLK)
            outs = []
            for s in range(2):
                cols = pl.ds(at + 128 * s, 128)
                mine = lane < 64 if s == 0 else lane >= 64
                base = 64 if s == 0 else 0
                qt = qx[rows, cols]
                diag = jnp.where(causal, nt(qt, kx[rows, cols]), masked_score)
                peak = jnp.max(diag, axis=-1, keepdims=True)
                if i > 0:
                    full = nt(qt, kx[0 : BLK * i, cols])
                    peak = jnp.maximum(peak, jnp.max(full, axis=-1, keepdims=True))
                vd = v[rows, pl.ds(vat, 128)]
                vd = jnp.where(mine, vd, jnp.ones_like(vd))
                o = nn(jnp.exp(diag - peak).astype(bf16), vd)
                if i > 0:
                    vf = v[0 : BLK * i, pl.ds(vat, 128)]
                    lf = lane_ids((BLK * i, 128))
                    vf = jnp.where(lf < 64 if s == 0 else lf >= 64, vf, jnp.ones_like(vf))
                    o = o + nn(jnp.exp(full - peak).astype(bf16), vf)
                outs.append(o / pltpu.roll(o, 64, 1))
                hi, mid_, lo = split3(-(peak + jnp.log(o)))
                qn = jnp.where(lane == base + 1, hi, qt.astype(f32))
                qn = jnp.where(lane == base + 2, mid_, qn)
                qn = jnp.where(lane == base + 3, lo, qn)
                qx[rows, cols] = qn.astype(bf16)
            ctx[rows, pl.ds(vat, 128)] = jnp.where(lane < 64, outs[0], outs[1]).astype(bf16)
        return 0

    lax.fori_loop(0, PAIRS, attend, 0)
    loads[3].wait()

    def finish(i, _):
        r = pl.multiple_of(i * BLK, BLK)
        rows = pl.ds(r, BLK)
        m = nn(ctx[rows, :], wp[...]) + pb[...].reshape(1, D) + x[rows, :].astype(f32)
        mid[rows, :] = m
        normed, _unused = row_stats(m)
        n2[rows, :] = (normed * gain2[...].reshape(1, D) + shift2[...].reshape(1, D)).astype(bf16)
        return 0

    lax.fori_loop(0, ROWS // BLK, finish, 0)
    late_out = [
        pltpu.make_async_copy(src, dst, out_sem.at[4 + i])
        for i, (src, dst) in enumerate(((qx, qx_h), (ctx, ctx_h), (mid, mid_h), (n2, n2_h)))
    ]
    for cp in late_out:
        cp.start()
    loads[2].wait()
    swaps[1].wait()
    fill(cot, cot_in)

    def turn(i, _):
        r = pl.multiple_of(i * BLK, BLK)
        cotr[pl.ds(r, BLK), :] = rotated(dbl, a, i).astype(bf16)
        return 0

    lax.fori_loop(0, ROWS // BLK, turn, 0)
    last = pltpu.make_async_copy(cotr, cotr_h, out_sem.at[8])
    last.start()
    for cp in early + late_out + [last]:
        cp.wait()


def forward_call(lens, tok, cot, gain1, shift1, wq, qb, vb, wp, pb, gain2, shift2):
    shapes = [
        ((ROWS, D), bf16),
        ((ROWS, D), bf16),
        ((ROWS, D), bf16),
        ((ROWS, 2 * D), bf16),
        ((ROWS, 2 * D), bf16),
        ((ROWS, D), bf16),
        ((ROWS, D), bf16),
        ((ROWS, D), f32),
        ((ROWS, D), bf16),
    ]
    x, cotr, n1, qx, kx, v, ctx, mid, n2 = [pltpu.VMEM(s, t) for s, t in shapes]
    return pl.pallas_call(
        forward_kernel,
        out_shape=[jax.ShapeDtypeStruct(s, t) for s, t in shapes],
        in_specs=[SMEM, ANY, ANY, VMEM, VMEM, ANY, VMEM, VMEM, ANY, VMEM, VMEM, VMEM],
        out_specs=[ANY] * 9,
        scratch_shapes=[
            pltpu.VMEM((ROWS, D), bf16), pltpu.VMEM((ROWS, D), bf16),
            pltpu.VMEM((SWAP, D), bf16), pltpu.VMEM((SWAP, D), bf16),
            pltpu.VMEM((ROWS, D), bf16),
            x, cotr, n1, qx, kx, v, ctx, mid, n2,
            pltpu.VMEM((D, 3 * D), bf16), pltpu.VMEM((D, D), bf16),
            pltpu.SemaphoreType.DMA((4,)), pltpu.SemaphoreType.DMA((2,)),
            pltpu.SemaphoreType.DMA((2,)), pltpu.SemaphoreType.DMA((9,)),
        ],
        compiler_params=pltpu.CompilerParams(
            collective_id=0, has_side_effects=True, vmem_limit_bytes=VMEM_LIMIT),
        cost_estimate=pl.CostEstimate(
            flops=14 * 10**9, bytes_accessed=30 * 10**6, transcendentals=8 * 10**6),
        name="forward",
    )(lens, tok, cot, gain1, shift1, wq, qb, vb, wp, pb, gain2, shift2)


def norm_back(v, gain, r):
    n, scale = row_stats(v)
    u = gain * r
    back = scale * (u - jnp.mean(u, axis=-1, keepdims=True) - n * jnp.mean(u * n, axis=-1, keepdims=True))
    return back, jnp.sum(r * n, axis=0, keepdims=True), jnp.sum(r, axis=0, keepdims=True)


def backward_kernel(
    nz, direct,
    lens, x_h, cot_h, n1_h, qx_h, kx_h, v_h, ctx_h, mid_h, n2_h,
    gain1, gain2, eb, sb, we_h, ws_h, wq_h, wp_h,
    *rest,
):
    n_out = 7 if direct else 5
    out_h, ig_h, vec_h = rest[:3]
    grads_h = rest[3:n_out]
    (gs, ge, cot, acc, dn, obuf, obuf_in, ibuf, ibuf_in, qx, kx, v, vec, vec_in, load_sem, out_sem,
     swap_send, swap_recv) = rest[n_out : n_out + 18]
    if direct:
        (r0s, r0e, r1s, r1e, r2s, r2e, r3s, r3e, oq, op, oe, os_,
         s_send, s_recv, e_send, e_recv, j_send, j_recv, v_send, v_recv) = rest[n_out + 18 :]
    b = lax.axis_index("batch")
    c = lax.axis_index("seq")
    a = lens[0, 0]
    xx = b % 2
    yy = (b // 2) % 2
    zz = b // 4
    partner = (b, 1 - c)
    xn = (b + 1 - 2 * xx, c)
    yn = (b + 2 - 4 * yy, c)
    n1st = (b + (1 - c) * (1 - 2 * xx) + c * (2 - 4 * yy), c)
    n2nd = (b + c * (1 - 2 * xx) + (1 - c) * (2 - 4 * yy), c)
    zpeers = [(zz + i) % nz for i in range(1, nz)] if direct else []
    keep = [(1 - c) * (2 * k + xx) + c * (2 * yy + k) for k in range(2)]
    give = [(1 - c) * (2 * k + 1 - xx) + c * (2 * (1 - yy) + k) for k in range(2)]
    give2 = (1 - c) * (2 * (1 - yy) + xx) + c * (2 * yy + 1 - xx)
    home = 2 * yy + xx
    friends = [partner]
    if direct:
        friends += [xn, yn] + [(b % 4 + 4 * z, c) for z in zpeers]

    def load(src, dst, i):
        return pltpu.make_async_copy(src, dst, load_sem.at[i])

    def remote(src, dst, send, recv, to):
        return pltpu.make_async_remote_copy(
            src_ref=src, dst_ref=dst, send_sem=send, recv_sem=recv,
            device_id=to, device_id_type=MESH)

    def copies(kind, u, stage):
        slot = u % 2
        if kind == "s":
            if stage == 0:
                return [remote(gs.at[1 - c, :, u], r0s.at[slot], s_send.at[u, 0], s_recv.at[u, 0], partner)]
            if stage == 1:
                return [remote(gs.at[c, give[k], u], r1s.at[slot, k], s_send.at[u, 1 + k], s_recv.at[u, 1 + k], n1st)
                        for k in range(2)]
            if stage == 2:
                return [remote(gs.at[c, give2, u], r2s.at[slot], s_send.at[u, 3], s_recv.at[u, 3], n2nd)]
            return [remote(gs.at[c, home, z], r3s.at[i], j_send.at[i], j_recv.at[i], (b % 4 + 4 * z, c))
                    for i, z in enumerate(zpeers)]
        if stage == 0:
            return [remote(ge.at[u, 1 - c], r0e.at[slot], e_send.at[u, 0], e_recv.at[u, 0], partner)]
        if stage == 1:
            return [remote(ge.at[u, c, give[k]], r1e.at[slot, k], e_send.at[u, 1 + k], e_recv.at[u, 1 + k], n1st)
                    for k in range(2)]
        if stage == 2:
            return [remote(ge.at[u, c, give2], r2e.at[slot], e_send.at[u, 3], e_recv.at[u, 3], n2nd)]
        return [remote(ge.at[u, c, home, z], r3e.at[u, i], e_send.at[u, 4 + i], e_recv.at[u, 4 + i],
                       (b % 4 + 4 * z, c)) for i, z in enumerate(zpeers)]

    def start(kind, u, stage):
        if direct:
            for cp in copies(kind, u, stage):
                cp.start()

    def finish(kind, u, stage):
        for cp in copies(kind, u, stage):
            cp.wait()

    def add_into(dst, src):
        dst[...] = (dst[...].astype(f32) + src[...].astype(f32)).astype(bf16)

    def advance(kind, u, stage):
        finish(kind, u, stage - 1)
        slot = u % 2
        if kind == "s":
            if stage == 1:
                for k in range(4):
                    add_into(gs.at[c, k, u], r0s.at[slot, k])
            elif stage == 2:
                for k in range(2):
                    add_into(gs.at[c, keep[k], u], r1s.at[slot, k])
            elif stage == 3:
                add_into(gs.at[c, home, u], r2s.at[slot])
        else:
            if stage == 1:
                for k in range(4):
                    add_into(ge.at[u, c, k], r0e.at[slot, k])
            elif stage == 2:
                for k in range(2):
                    add_into(ge.at[u, c, keep[k]], r1e.at[slot, k])
            elif stage == 3:
                add_into(ge.at[u, c, home], r2e.at[slot])
        if kind == "e" or stage < 3:
            start(kind, u, stage)

    def settle(kind, u):
        finish(kind, u, 3)
        if kind == "s":
            total = gs[c, home, zz].astype(f32)
            for i in range(nz - 1):
                total = total + r3s[i].astype(f32)
            os_[...] = total
            return
        total = ge[u, c, home, zz].astype(f32)
        for i in range(nz - 1):
            total = total + r3e[u, i].astype(f32)
        for h in range(2):
            half = total[24 * h : 24 * h + 24, :]
            if u < 4:
                oe[:, 768 * u + 384 * h : 768 * u + 384 * h + 384] = half
            elif u == 4:
                op[:, 384 * h : 384 * h + 384] = half
            else:
                for w in range(3):
                    at = 768 * w + 256 * (u - 5) + 128 * h
                    oq[:, at : at + 128] = half[:, 128 * w : 128 * w + 128]

    plan = {}
    for j in range(4):
        plan.setdefault(j + 1, []).extend([(1, "s", j), (1, "e", j)])
        plan.setdefault(j + 2, []).extend([(2, "s", j), (2, "e", j)])
        plan.setdefault(j + 3, []).extend([(3, "s", j), (3, "e", j)])
        plan.setdefault(j + 4, []).append((4, "e", j))
    plan.setdefault(7, []).append((5, "s", 0))
    plan.setdefault(9, []).append((6, "s", 0))
    for u, t in ((4, 4), (5, 6), (6, 8), (7, 10)):
        for stage in range(1, 5):
            plan.setdefault(t + stage, []).append((stage, "e", u))

    def tick(t, now=None):
        if not direct:
            return

        def act():
            for stage, kind, u in sorted(plan.get(t, []), key=lambda e: -e[0]):
                if stage == 6 or (stage == 4 and kind == "e"):
                    settle(kind, u)
                elif stage == 5:
                    start("s", 0, 3)
                else:
                    advance(kind, u, stage)

        if plan.get(t):
            if now is None:
                act()
            else:
                pl.when(now == t)(act)

    barrier = pltpu.get_barrier_semaphore()
    for f in friends:
        pl.semaphore_signal(barrier, inc=1, device_id=f, device_id_type=MESH)
    first = [load(cot_h, cot, 0), load(mid_h, acc, 1), load(qx_h, qx, 2), load(kx_h, kx, 3), load(v_h, v, 4)]
    pl.semaphore_wait(barrier, len(friends))
    vec[...] = jnp.zeros_like(vec)
    chunk = FF // 4

    def feed_forward(we, ws, n2, n2t, at, de):
        own = [load(n2_h, n2, 5), load(we_h, we, 6), load(ws_h, ws, 7)]
        for cp in own + first:
            cp.start()
        own[0].wait()

        def turn(i, _):
            r = pl.multiple_of(i * BLK, BLK)
            n2t[:, pl.ds(r, BLK)] = n2[pl.ds(r, BLK), :].T
            return 0

        lax.fori_loop(0, ROWS // BLK, turn, 0)
        for cp in own[1:] + first[:2]:
            cp.wait()

        def one(j, _):
            cols = pl.ds(pl.multiple_of(j * chunk, chunk), chunk)

            def tile(t, bias_sum):
                r = pl.multiple_of(t * BLK, BLK)
                rows = pl.ds(r, BLK)
                e = nn(n2[rows, :], we[:, cols]) + eb[cols].reshape(1, chunk)
                sq = e * e
                th = jnp.tanh(GELU_C * e * (1.0 + 0.044715 * sq))
                half = 0.5 * (1.0 + th)
                low = (e * half).astype(bf16)
                slope = half + (0.5 * GELU_C) * e * (1.0 - th * th) * (1.0 + (3 * 0.044715) * sq)
                grad = (nt(cot[rows, :], ws[cols, :]) * slope).astype(bf16)
                at[:, rows] = low.T
                de[rows, :] = grad
                acc[rows, :] += nn(low, ws[cols, :])
                part = nt(grad, we[:, cols])
                dn[rows, :] = jnp.where(j == 0, part, dn[rows, :] + part)
                return bias_sum + jnp.sum(grad.astype(f32), axis=0, keepdims=True)

            bias_sum = lax.fori_loop(0, ROWS // BLK, tile, jnp.zeros((1, chunk), f32))
            vec[pl.ds(8 + j, 1), :] = bias_sum
            for t in range(1, 4):
                tick(t, j)

            def shrink_part(i, _):
                r = pl.multiple_of(i * 192, 64)
                g = nn(at[pl.ds(r, 192), :], cot[...]).astype(bf16)
                for h in range(2):
                    gs[h, i, j] = g[96 * h : 96 * h + 96, :]
                return 0

            lax.fori_loop(0, 4, shrink_part, 0)
            start("s", j, 0)

            def expand_part(i, _):
                r = pl.multiple_of(i * 192, 64)
                g = nn(n2t[pl.ds(r, 192), :], de[...])
                for w in range(8):
                    q = g[24 * w : 24 * w + 24, :]
                    q = jnp.concatenate([q[:, 0:384], q[:, 384:768]], axis=0).astype(bf16)
                    ge[j, w % 2, w // 2, i] = q
                return 0

            lax.fori_loop(0, 4, expand_part, 0)
            start("e", j, 0)
            return 0

        lax.fori_loop(0, 4, one, 0)

    pl.run_scoped(
        feed_forward, pltpu.VMEM((D, FF), bf16), pltpu.VMEM((FF, D), bf16), pltpu.VMEM((ROWS, D), bf16),
        pltpu.VMEM((D, ROWS), bf16), pltpu.VMEM((chunk, ROWS), bf16), pltpu.VMEM((ROWS, chunk), bf16))
    tick(4)

    def unroll(dbl, buf):
        def step(i, _):
            r = pl.multiple_of(i * BLK, BLK)
            buf[pl.ds(r, BLK), :] = rotated(dbl, ROWS - a, i).astype(bf16)
            return 0

        lax.fori_loop(0, ROWS // BLK, step, 0)

    out_swap = remote(obuf.at[pl.ds(0, SWAP)], obuf_in, swap_send.at[0], swap_recv.at[0], partner)
    ig_swap = remote(ibuf.at[pl.ds(0, SWAP)], ibuf_in, swap_send.at[1], swap_recv.at[1], partner)
    lane = lane_ids((BLK, 128))

    def middle(dox):
        def second(mid, ctx, wp, dbl, gat):
            own = [load(mid_h, mid, 5), load(ctx_h, ctx, 6), load(wp_h, wp, 7)]
            for cp in own:
                cp.start()
            for cp in own:
                cp.wait()

            def tile(i, sums):
                r = pl.multiple_of(i * BLK, BLK)
                rows = pl.ds(r, BLK)
                dbl[rows, :] = (acc[rows, :] + sb[...].reshape(1, D)).astype(bf16)
                back, dgain, dshift = norm_back(mid[rows, :], gain2[...].reshape(1, D), dn[rows, :])
                ct = cot[rows, :].astype(f32)
                dmid = ct + back
                dn[rows, :] = dmid
                ga = dmid.astype(bf16)
                gat[rows, :] = ga
                dc = nt(ga, wp[...]).astype(bf16).astype(f32)
                cx = ctx[rows, :].astype(f32)
                for p in range(PAIRS):
                    d = dc[:, 128 * p : 128 * p + 128]
                    prod = d * cx[:, 128 * p : 128 * p + 128]
                    for s in range(2):
                        mine = lane < 64 if s == 0 else lane >= 64
                        base = 64 if s == 0 else 0
                        inner = jnp.sum(jnp.where(mine, prod, 0.0), axis=-1, keepdims=True)
                        hi, mid_, lo = split3(-inner)
                        aug = jnp.where(lane == base, hi, 0.0)
                        aug = jnp.where(lane == base + 1, mid_, aug)
                        aug = jnp.where(lane == base + 2, lo, aug)
                        at = 256 * p + 128 * s
                        dox[rows, at : at + 128] = jnp.where(mine, d, aug).astype(bf16)
                dpb = jnp.sum(ga.astype(f32), axis=0, keepdims=True)
                dsb = jnp.sum(ct, axis=0, keepdims=True)
                return tuple(o + n for o, n in zip(sums, (dgain, dshift, dpb, dsb)))

            zero = jnp.zeros((1, D), f32)
            sums = lax.fori_loop(0, ROWS // BLK, tile, (zero,) * 4)
            for at, s in zip((5, 6, 4, 7), sums):
                vec[at : at + 1, :] = s
            unroll(dbl, obuf)
            out_swap.start()

            def proj_part(i, _):
                r = pl.multiple_of(i * 192, 64)
                g = lax.dot_general(ctx[:, pl.ds(pl.multiple_of(i * 384, 128), 384)], gat[...],
                                    (((0,), (0,)), ((), ())), preferred_element_type=f32)
                for w in range(16):
                    q = g[24 * w : 24 * w + 24, :]
                    q = jnp.concatenate([q[:, 0:384], q[:, 384:768]], axis=0).astype(bf16)
                    ge[4, w % 2, (w // 2) % 4, 2 * i + w // 8] = q
                return 0

            lax.fori_loop(0, 2, proj_part, 0)
            start("e", 4, 0)

        pl.run_scoped(
            second, pltpu.VMEM((ROWS, D), f32), pltpu.VMEM((ROWS, D), bf16), pltpu.VMEM((D, D), bf16),
            pltpu.VMEM((ROWS, D), bf16), pltpu.VMEM((ROWS, D), bf16))
        return dox

    triangle = row_ids((BLK, BLK)) <= lane_ids((BLK, BLK))

    def attention(dox, dqkv, n1t, wq, x):
        later = [load(wq_h, wq, 5), load(x_h, x, 6)]
        for cp in later:
            cp.start()

        def attention_loop(n1, ktr, dqt):
            ln1 = load(n1_h, n1, 7)
            ln1.start()
            for cp in first[2:]:
                cp.wait()
            ln1.wait()

            def turn(i, _):
                r = pl.multiple_of(i * BLK, BLK)
                n1t[:, pl.ds(r, BLK)] = n1[pl.ds(r, BLK), :].T
                return 0

            lax.fori_loop(0, ROWS // BLK, turn, 0)

            def pair(p, _):
                at = pl.multiple_of(p * 256, 256)
                pat = pl.multiple_of(p * 128, 128)
                lf = lane_ids((ROWS, 128))
                kp = jnp.where(lf < 64, kx[:, pl.ds(at, 128)], kx[:, pl.ds(at + 128, 128)])
                ktr[...] = kp.T
                dqt[...] = jnp.zeros_like(dqt)
                dv_sum = jnp.zeros((1, 128), f32)
                for kb in range(ROWS // BLK):
                    krows = slice(BLK * kb, BLK * kb + BLK)
                    dks, dvs = [], []
                    for s in range(2):
                        cols = pl.ds(at + 128 * s, 128)
                        mine = lane < 64 if s == 0 else lane >= 64
                        vd = v[krows, pl.ds(pat, 128)]
                        vd = jnp.where(mine, vd, jnp.ones_like(vd))
                        kd = kx[krows, cols]
                        dk = jnp.zeros((BLK, 128), f32)
                        dv = jnp.zeros((BLK, 128), f32)
                        for qi in range(kb, ROWS // BLK):
                            qrows = slice(BLK * qi, BLK * qi + BLK)
                            qt = qx[qrows, cols]
                            dt = dox[qrows, cols]
                            prob = jnp.exp(nt(kd, qt))
                            if qi == kb:
                                prob = jnp.where(triangle, prob, 0.0)
                            ds = (prob * nt(vd, dt)).astype(bf16)
                            dv = dv + nn(prob.astype(bf16), dt)
                            dk = dk + nn(ds, qt)
                            dqt[64 * s : 64 * s + 64, qrows] += nn(ktr[64 * s : 64 * s + 64, krows], ds)
                        dks.append(dk)
                        dvs.append(dv)
                    dqkv[krows, pl.ds(D + pat, 128)] = jnp.where(lane < 64, dks[0], dks[1]).astype(bf16)
                    dvp = jnp.where(lane < 64, dvs[0], dvs[1]).astype(bf16)
                    dqkv[krows, pl.ds(2 * D + pat, 128)] = dvp
                    dv_sum = dv_sum + jnp.sum(dvp.astype(f32), axis=0, keepdims=True)
                dq = (dqt[...] * 0.125).astype(bf16).T
                dqkv[:, pl.ds(pat, 128)] = dq
                vec[2:3, pl.ds(pat, 128)] = jnp.sum(dq.astype(f32), axis=0, keepdims=True)
                vec[3:4, pl.ds(pat, 128)] = dv_sum
                for t in range(5, 11):
                    tick(t, p + 5)

                @pl.when(p % 2 == 1)
                def _():
                    k = p // 2

                    def qkv_part(i, _):
                        r = pl.multiple_of(i * 384, 128)
                        for w in range(3):
                            g = nn(n1t[pl.ds(r, 384), :], dqkv[:, pl.ds(pl.multiple_of(768 * w + 256 * k, 256), 256)])
                            for q_ in range(16):
                                q = g[24 * q_ : 24 * q_ + 24, :]
                                q = jnp.concatenate([q[:, 0:128], q[:, 128:256]], axis=0).astype(bf16)
                                ge[5 + k, q_ % 2, (q_ // 2) % 4, 2 * i + q_ // 8, :, 128 * w : 128 * w + 128] = q
                        return 0

                    lax.fori_loop(0, 2, qkv_part, 0)
                    start("e", 5 + k, 0)

                return 0

            lax.fori_loop(0, PAIRS, pair, 0)

        pl.run_scoped(
            attention_loop, pltpu.VMEM((ROWS, D), bf16), pltpu.VMEM((128, ROWS), bf16), pltpu.VMEM((128, ROWS), f32))
        for cp in later:
            cp.wait()

        def tail(dbl):
            def tile(i, sums):
                r = pl.multiple_of(i * BLK, BLK)
                rows = pl.ds(r, BLK)
                g = nt(dqkv[rows, :], wq[...])
                back, dgain, dshift = norm_back(x[rows, :].astype(f32), gain1[...].reshape(1, D), g)
                dbl[rows, :] = (dn[rows, :] + back).astype(bf16)
                for t in range(11, 15):
                    tick(t, i + 11)
                return sums[0] + dgain, sums[1] + dshift

            zero = jnp.zeros((1, D), f32)
            sums = lax.fori_loop(0, ROWS // BLK, tile, (zero,) * 2)
            vec[0:1, :] = sums[0]
            vec[1:2, :] = sums[1]
            unroll(dbl, ibuf)
            ig_swap.start()

        pl.run_scoped(tail, pltpu.VMEM((ROWS, D), bf16))

    def both(dox):
        middle(dox)
        pl.run_scoped(
            functools.partial(attention, dox), pltpu.VMEM((ROWS, 3 * D), bf16), pltpu.VMEM((D, ROWS), bf16),
            pltpu.VMEM((D, 3 * D), bf16), pltpu.VMEM((ROWS, D), bf16))

    pl.run_scoped(both, pltpu.VMEM((ROWS, 2 * D), bf16))

    outs = []

    def emit(src, dst):
        cp = pltpu.make_async_copy(src, dst, out_sem.at[len(outs)])
        cp.start()
        outs.append(cp)

    if direct:
        at = 0
        for group in ([partner], [xn], [yn], [(b % 4 + 4 * z, c) for z in zpeers]):
            cps = [remote(vec, vec_in.at[at + i], v_send.at[at + i], v_recv.at[at + i], to)
                   for i, to in enumerate(group)]
            for cp in cps:
                cp.start()
            for cp in cps:
                cp.wait()
            total = vec[...]
            for i in range(len(group)):
                total = total + vec_in[at + i]
            vec[...] = total
            at += len(group)
        emit(vec, vec_h)
        for src, dst in zip((oq, op, oe, os_), grads_h):
            emit(src, dst)
    else:
        emit(vec, vec_h)
        emit(gs, grads_h[0])
        emit(ge, grads_h[1])

    def give_back(swap, buf, buf_in, final):
        swap.wait()

        def step(i, _):
            r = pl.multiple_of(i * BLK, BLK)
            rows = pl.ds(r, BLK)
            own = buf[rows, :].astype(f32)
            other = buf_in[rows, :].astype(f32)
            final[rows, :] = jnp.where(row_ids((BLK, D)) + r >= a, own, other).astype(final.dtype)
            return 0

        lax.fori_loop(0, SWAP // BLK, step, 0)
        final[SWAP:ROWS, :] = buf[SWAP:ROWS, :].astype(final.dtype)

    give_back(out_swap, obuf, obuf_in, cot)
    emit(cot, out_h)
    give_back(ig_swap, ibuf, ibuf_in, acc)
    emit(acc, ig_h)
    for cp in outs:
        cp.wait()


def backward_call(nz, direct, *args):
    unit = (48, 384)
    if direct:
        grads = [((24, 3 * D), f32), ((24, D), f32), ((24, FF), f32), ((96, D), f32)]
    else:
        grads = [((2, 4, 4, 96, D), bf16), ((8, 2, 4, 4) + unit, bf16)]
    shapes = [((ROWS, D), bf16), ((ROWS, D), f32), ((16, D), f32)] + grads
    scratch = [
        pltpu.VMEM((2, 4, 4, 96, D), bf16), pltpu.VMEM((8, 2, 4, 4) + unit, bf16),
        pltpu.VMEM((ROWS, D), bf16), pltpu.VMEM((ROWS, D), f32), pltpu.VMEM((ROWS, D), f32),
        pltpu.VMEM((ROWS, D), bf16), pltpu.VMEM((SWAP, D), bf16),
        pltpu.VMEM((ROWS, D), bf16), pltpu.VMEM((SWAP, D), bf16),
        pltpu.VMEM((ROWS, 2 * D), bf16), pltpu.VMEM((ROWS, 2 * D), bf16), pltpu.VMEM((ROWS, D), bf16),
        pltpu.VMEM((16, D), f32), pltpu.VMEM((6, 16, D), f32),
        pltpu.SemaphoreType.DMA((8,)), pltpu.SemaphoreType.DMA((8,)),
        pltpu.SemaphoreType.DMA((2,)), pltpu.SemaphoreType.DMA((2,)),
    ]
    if direct:
        scratch += [
            pltpu.VMEM((2, 4, 96, D), bf16), pltpu.VMEM((2, 4, nz) + unit, bf16),
            pltpu.VMEM((2, 2, 96, D), bf16), pltpu.VMEM((2, 2, nz) + unit, bf16),
            pltpu.VMEM((2, 96, D), bf16), pltpu.VMEM((2, nz) + unit, bf16),
            pltpu.VMEM((nz - 1, 96, D), bf16), pltpu.VMEM((8, nz - 1) + unit, bf16),
            pltpu.VMEM((24, 3 * D), f32), pltpu.VMEM((24, D), f32), pltpu.VMEM((24, FF), f32), pltpu.VMEM((96, D), f32),
            pltpu.SemaphoreType.DMA((4, 4)), pltpu.SemaphoreType.DMA((4, 4)),
            pltpu.SemaphoreType.DMA((8, 7)), pltpu.SemaphoreType.DMA((8, 7)),
            pltpu.SemaphoreType.DMA((3,)), pltpu.SemaphoreType.DMA((3,)),
            pltpu.SemaphoreType.DMA((6,)), pltpu.SemaphoreType.DMA((6,)),
        ]
    return pl.pallas_call(
        functools.partial(backward_kernel, nz, direct),
        out_shape=[jax.ShapeDtypeStruct(s, t) for s, t in shapes],
        in_specs=[SMEM] + [ANY] * 9 + [VMEM] * 4 + [ANY] * 4,
        out_specs=[ANY] * len(shapes),
        scratch_shapes=scratch,
        compiler_params=pltpu.CompilerParams(
            collective_id=1, has_side_effects=True, vmem_limit_bytes=VMEM_LIMIT),
        cost_estimate=pl.CostEstimate(
            flops=50 * 10**9, bytes_accessed=50 * 10**6, transcendentals=12 * 10**6),
        name="backward",
    )(*args)


def on_device(nz, direct, tokens, lens, gain1, shift1, wq, qb, vb, wp, pb, gain2, shift2, we, eb, ws, sb, cot):
    x, cotr, n1, qx, kx, v, ctx, mid, n2 = forward_call(
        lens, tokens, cot, gain1, shift1, wq, qb, vb, wp, pb, gain2, shift2)
    out, ig, vec, *grads = backward_call(
        nz, direct, lens, x, cotr, n1, qx, kx, v, ctx, mid, n2, gain1, gain2, eb, sb, we, ws, wq, wp)
    shards = lax.axis_size("batch") * 2
    me = lax.axis_index("batch") * 2 + lax.axis_index("seq")

    if direct:
        gq, gp, ge, gs = grads

        def own_part(row, rows=1):
            flat = vec[row : row + rows].reshape(rows * D)
            n = rows * D // shards
            return lax.dynamic_slice(flat, (me * n,), (n,))
    else:
        def scatter(g):
            return lax.psum_scatter(g, ("batch", "seq"), scatter_dimension=0, tiled=True)

        def own_part(row, rows=1):
            return scatter(vec[row : row + rows].reshape(rows * D))

        us, ue = (g.astype(f32) for g in grads)
        gs = scatter(us.transpose(2, 1, 0, 3, 4).reshape(FF, D))
        ue = ue.reshape(8, 2, 4, 4, 2, 24, 384)
        wide = ue[:5].transpose(3, 2, 1, 5, 0, 4, 6).reshape(D, 5 * D)
        ge = scatter(wide[:, :FF])
        gp = scatter(wide[:, FF:])
        gq = ue[5:].reshape(3, 2, 4, 4, 2, 24, 3, 128).transpose(3, 2, 1, 5, 6, 0, 4, 7).reshape(D, 3 * D)
        gq = scatter(gq)
    return (out, ig, own_part(0), own_part(1), gq, own_part(2), own_part(3), gp, own_part(4),
            own_part(5), own_part(6), ge, own_part(8, 4), gs, own_part(7))


def solution(mesh):
    nz = mesh.shape["batch"] // 4
    direct = mesh.shape["batch"] == 16 and mesh.shape["seq"] == 2
    rows = P(("batch", "seq"), None)
    part = P(("batch", "seq"))
    whole = P()
    in_specs = (rows, P("batch", None)) + (whole,) * 13 + (rows,)
    out_specs = (rows, rows, part, part, rows, part, part, rows, part, part, part, rows, part, rows, part)
    return jax.shard_map(
        functools.partial(on_device, nz, direct),
        mesh=mesh, in_specs=in_specs, out_specs=out_specs, check_vma=False)
```

time: 903 us -> 225 us (0.25)
  matrix products: 292 us -> 0 us
  waiting for transfers between devices: 282 us -> 0 us
  Pallas kernels: 0 us -> 212 us
  local copies, waits for them, and re-layouts: 140 us -> 12.1 us
  other arithmetic: 94.7 us -> 0 us
  blocking collectives: 57.7 us -> 0 us
  between operations: 16.5 us -> 0.7 us
  starting transfers between devices: 11.1 us -> 0 us
    reduce_scatter x4 -> x0, waiting for transfers between devices: 281 us -> none  [the longest x1 142 us: on_device(): lax.psum_scatter(grad_expand_weight, ('batch', 'seq'), scatter_dimension=...]
    dot_general x32 -> x0, matrix products: 240 us -> none  [the longest x4 44.8 us: on_device(): jnp.einsum('qhd,khd->hqk', grad_block, value_all[:extent], preferred_elem...]
    pallas_call x0 -> x2, Pallas kernels: none -> 212 us  [the longest x1 168 us: backward_call(): pl.pallas_call(functools.partial(backward_kernel, nz, direct), out_shape=...]
    sub x4 -> x0, matrix products: 51.9 us -> none  [on_device(): weights = jnp.exp(scores - row_peak)]
    convert_element_type x5 -> x0, other arithmetic: 45.2 us -> none  [the longest x4 44.7 us: on_device(): grad_scores = (softmax_f * (grad_weights - row_inner)).astype(jnp.bfloat16)]
    unnamed x1 -> x0, blocking collectives: 43.8 us -> none
    slice x19 -> x2, local copies, waits for them, and re-layouts: 33.4 us -> 1.92 us  [own_part(): flat = vec[row:row + rows].reshape(rows * D)]
    another operation x3 -> x0, local copies, waits for them, and re-layouts: 25.9 us -> none  [on_device(): jnp.stack([grad_queries, grad_keys.reshape(group_rows, local_width), grad...]
  transfers between devices with their start and end apart: 6 -> 0, of which waited for: 3 -> 0; matrix products, arithmetic and copies ran while one was open for 33% -> 0% of each run, Pallas kernels for 0% -> 0%
where the time goes in v1:
time: 225 us
  Pallas kernels  212 us (94%)
  local copies, waits for them, and re-layouts  12.1 us (5%)
    pallas_call x1, Pallas kernels, backward_call(): pl.pallas_call(functools.partial(backward_kernel, nz, direct), out_shape=...  168 us
    pallas_call x1, Pallas kernels, forward_call(): pl.pallas_call(forward_kernel, out_shape=[jax.ShapeDtypeStruct(s, t) for...  43.9 us
    unnamed x16, local copies, waits for them, and re-layouts  7.23 us

profile of v1, /device:TPU:0, one launch (start us, length us, event | category | flops | bytes accessed | tf_op | source)
XLA Modules:
  0.0 224.6 jit_solution(16075318757428080318)
XLA Ops:
  0.6 43.9 %forward.1 = (bf16[1024,768]{1,0:T(8,128)(2,1)}, bf16[1024,768]{1,0:T(8,128)(2,1)}, bf16[1024,768]{1,0:T(8,128)(2,1)}, bf16[1024,1536]{1,0:T(8,128)(2,1)}, bf16[...) custom-call(s32[1,3]{1,0:T(1,128)} %lens.3, ...), custom_call_target="tpu_custom_call" | custom-call | flops 14000000000 | bytes 30000000 | tf_op jit(solution)/shard_map/forward/pallas_call | solution.py:246
  44.5 167.9 %backward.1 = (bf16[1024,768]{1,0:T(8,128)(2,1)}, f32[1024,768]{1,0:T(8,128)}, f32[16,768]{1,0:T(8,128)}, f32[24,2304]{1,0:T(8,128)}, f32[24,768]{1,0:T(8,128)}, /*index=5*/f32[24,3072]{1,0:T(8,128)}, f32[96,768]{1,0:T(8,128)}) custom-call(s32[1,3]{1,0:T(1,128)} %lens.3, bf16[1024,768]{1,0:T(8,128)(2,1)} %get-tuple-element.31.x_h, ...), custom_call_target="tpu_custom_call" | custom-call | flops 49999998976 | bytes 50000000 | tf_op jit(solution)/shard_map/backward/pallas_call | solution.py:778
  212.5 1.2 fusion.8
  213.6 0.6 fusion.6
  214.2 0.6 fusion.4
  214.8 0.6 fusion.2
  215.4 0.6 fusion
  216.0 0.7 slice.34
  216.7 0.6 dynamic_slice.57
  217.3 0.0 copy-start
  217.3 2.8 %copy.37 = bf16[1024,768]{1,0:T(8,128)(2,1)} copy(bf16[1024,768]{1,0:T(8,128)(2,1)} %get-tuple-element.78) | data formatting | bytes 3145728
  220.1 0.0 copy-done
  220.1 0.0 copy-start.3
  220.1 0.0 copy-start.4
  220.1 0.0 copy-start.2
  220.2 0.0 copy-start.1
  220.2 1.7 copy.38
  221.8 0.0 copy-done.3
  221.8 0.7 copy.39
  222.5 0.0 copy-done.4
  222.5 0.6 copy.40
  223.2 0.0 copy-done.2
  223.2 0.7 copy.41
  223.9 0.0 copy-done.1
  223.9 0.7 copy.42
  (1 shorter events, 0.0 us)
Async XLA Ops:
  217.3 2.8 %copy-start = (f32[1024,768]{1,0:T(8,128)S(1)}, f32[1024,768]{1,0:T(8,128)}, u32[]{:S(2)}) copy-start(f32[1024,768]{1,0:T(8,128)} %get-tuple-element.79) | copy-start | bytes 9437188
  220.1 1.7 copy-start.3
  220.1 2.4 %copy-start.4 = (f32[24,768]{1,0:T(8,128)S(1)}, f32[24,768]{1,0:T(8,128)}, u32[]{:S(2)}) copy-start(f32[24,768]{1,0:T(8,128)} %get-tuple-element.85) | copy-start | bytes 221188
  220.1 3.0 %copy-start.2 = (f32[24,3072]{1,0:T(8,128)S(1)}, f32[24,3072]{1,0:T(8,128)}, u32[]{:S(2)}) copy-start(f32[24,3072]{1,0:T(8,128)} %get-tuple-element.89) | copy-start | bytes 884740
  220.2 3.7 %copy-start.1 = (f32[96,768]{1,0:T(8,128)S(1)}, f32[96,768]{1,0:T(8,128)}, u32[]{:S(2)}) copy-start(f32[96,768]{1,0:T(8,128)} %get-tuple-element.91) | copy-start | bytes 884740

commit v2 on v1

v2 whole, which is shorter than its diff:
```python
import functools
import math

import jax
import jax.numpy as jnp
from jax import lax
from jax.experimental import pallas as pl
from jax.experimental.pallas import tpu as pltpu
from jax.sharding import PartitionSpec as P

f32 = jnp.float32
bf16 = jnp.bfloat16
MESH = pl.DeviceIdType.MESH
ANY = pl.BlockSpec(memory_space=pl.ANY)
VMEM = pl.BlockSpec(memory_space=pltpu.VMEM)
SMEM = pl.BlockSpec(memory_space=pltpu.SMEM)

H = 12
epsilon = 1e-05
masked_score = -1e30
ROWS = 1024
SWAP = 768
D = 768
FF = 3072
PAIRS = 6
BLK = 256
VMEM_LIMIT = 63 * 2**20
GELU_C = 0.7978845608028654


def nn(a, b):
    return lax.dot_general(a, b, (((1,), (0,)), ((), ())), preferred_element_type=f32)


def nt(a, b):
    return lax.dot_general(a, b, (((1,), (1,)), ((), ())), preferred_element_type=f32)


def tn(a, b):
    return lax.dot_general(a, b, (((0,), (0,)), ((), ())), preferred_element_type=f32)


def row_stats(v):
    mean = jnp.mean(v, axis=-1, keepdims=True)
    centered = v - mean
    var = jnp.mean(centered * centered, axis=-1, keepdims=True)
    return centered * lax.rsqrt(var + epsilon), lax.rsqrt(var + epsilon)


def lane_ids(shape):
    return lax.broadcasted_iota(jnp.int32, shape, 1)


def row_ids(shape):
    return lax.broadcasted_iota(jnp.int32, shape, 0)


def split3(v):
    hi = v.astype(bf16).astype(f32)
    rest = v - hi
    mid = rest.astype(bf16).astype(f32)
    return hi, mid, rest - mid


def rotated(m, shift, i):
    coarse = lax.shift_right_logical(shift, 8)
    fine = lax.bitwise_and(shift, 255)

    def two(k):
        blocks = [m[pl.ds(pl.multiple_of(((i + k + n) % 4) * BLK, BLK), BLK), :] for n in range(2)]
        return jnp.concatenate(blocks, axis=0)

    part = jnp.where(coarse == 1, two(1), jnp.where(coarse == 2, two(2), two(3)))
    shape = (BLK, 2 * BLK)
    pick = (lane_ids(shape) == row_ids(shape) + fine).astype(f32).astype(bf16)
    return nn(pick, part)


def norm_back(v, gain, r):
    n, scale = row_stats(v)
    u = gain * r
    back = scale * (u - jnp.mean(u, axis=-1, keepdims=True) - n * jnp.mean(u * n, axis=-1, keepdims=True))
    return back, jnp.sum(r * n, axis=0, keepdims=True), jnp.sum(r, axis=0, keepdims=True)


def gelu_parts(e):
    sq = e * e
    th = jnp.tanh(e * (GELU_C + (GELU_C * 0.044715) * sq))
    half = 0.5 + 0.5 * th
    slope = half + (e * (1.0 - th * th)) * (0.5 * GELU_C + (1.5 * GELU_C * 0.044715) * sq)
    return e * half, slope


def spare_rows(*rows):
    ids = row_ids((64, rows[0].shape[1]))
    out = jnp.zeros(ids.shape, f32)
    for i, row in enumerate(rows):
        out = jnp.where(ids == i, row, out)
    return out


def with_spare(s, part, spare):
    return jnp.concatenate([part, spare] if s == 0 else [spare, part], axis=0).astype(bf16)


def layer_kernel(
    nz, direct,
    lens, tok_h, cot_h, gain1, shift1, wq_h, qb, vb, wp_h, pb, gain2, shift2, we_h, eb, ws_h, sb,
    *rest,
):
    n_out = 10 if direct else 8
    out_h, out_in_h, ig_h, ig_in_h, vec_h, mid_h = rest[:6]
    grads_h = rest[6:n_out]
    (gs, ge, tok_in, cot_in, m, cot, x, n1, q, qxt, kx, v, ctxt, acc, dn, n2, wq, wp, lse, vec, vec_in,
     load_sem, out_sem, swap_send, swap_recv) = rest[n_out : n_out + 25]
    if direct:
        (r0s, r0e, r1s, r1e, r2s, r2e, r3s, r3e, oq, op, oe, os_,
         s_send, s_recv, e_send, e_recv, j_send, j_recv, v_send, v_recv) = rest[n_out + 25 :]
    b = lax.axis_index("batch")
    c = lax.axis_index("seq")
    a = lens[0, 0]
    xx = b % 2
    yy = (b // 2) % 2
    zz = b // 4
    partner = (b, 1 - c)
    xn = (b + 1 - 2 * xx, c)
    yn = (b + 2 - 4 * yy, c)
    n1st = (b + (1 - c) * (1 - 2 * xx) + c * (2 - 4 * yy), c)
    n2nd = (b + c * (1 - 2 * xx) + (1 - c) * (2 - 4 * yy), c)
    zpeers = [(zz + i) % nz for i in range(1, nz)] if direct else []
    keep = [(1 - c) * (2 * k + xx) + c * (2 * yy + k) for k in range(2)]
    give = [(1 - c) * (2 * k + 1 - xx) + c * (2 * (1 - yy) + k) for k in range(2)]
    give2 = (1 - c) * (2 * (1 - yy) + xx) + c * (2 * yy + 1 - xx)
    home = 2 * yy + xx
    friends = [partner]
    if direct:
        friends += [xn, yn] + [(b % 4 + 4 * z, c) for z in zpeers]

    def load(src, dst, i):
        return pltpu.make_async_copy(src, dst, load_sem.at[i])

    def remote(src, dst, send, recv, to):
        return pltpu.make_async_remote_copy(
            src_ref=src, dst_ref=dst, send_sem=send, recv_sem=recv,
            device_id=to, device_id_type=MESH)

    def place(u):
        return u if not direct else u % 5

    def copies(kind, u, stage):
        slot = u % 2
        if kind == "s":
            if stage == 0:
                return [remote(gs.at[1 - c, :, u], r0s.at[slot], s_send.at[u, 0], s_recv.at[u, 0], partner)]
            if stage == 1:
                return [remote(gs.at[c, give[k], u], r1s.at[slot, k], s_send.at[u, 1 + k], s_recv.at[u, 1 + k], n1st)
                        for k in range(2)]
            if stage == 2:
                return [remote(gs.at[c, give2, u], r2s.at[slot], s_send.at[u, 3], s_recv.at[u, 3], n2nd)]
            return [remote(gs.at[c, home, z], r3s.at[i], j_send.at[i], j_recv.at[i], (b % 4 + 4 * z, c))
                    for i, z in enumerate(zpeers)]
        g = ge.at[place(u)]
        if stage == 0:
            return [remote(g.at[1 - c], r0e.at[slot], e_send.at[u, 0], e_recv.at[u, 0], partner)]
        if stage == 1:
            return [remote(g.at[c, give[k]], r1e.at[slot, k], e_send.at[u, 1 + k], e_recv.at[u, 1 + k], n1st)
                    for k in range(2)]
        if stage == 2:
            return [remote(g.at[c, give2], r2e.at[slot], e_send.at[u, 3], e_recv.at[u, 3], n2nd)]
        return [remote(g.at[c, home, z], r3e.at[u, i], e_send.at[u, 4 + i], e_recv.at[u, 4 + i],
                       (b % 4 + 4 * z, c)) for i, z in enumerate(zpeers)]

    def start(kind, u, stage):
        if direct:
            for cp in copies(kind, u, stage):
                cp.start()

    def finish(kind, u, stage):
        for cp in copies(kind, u, stage):
            cp.wait()

    def add_into(dst, src):
        dst[...] = (dst[...].astype(f32) + src[...].astype(f32)).astype(bf16)

    def advance(kind, u, stage):
        finish(kind, u, stage - 1)
        slot = u % 2
        if kind == "s":
            if stage == 1:
                for k in range(4):
                    add_into(gs.at[c, k, u], r0s.at[slot, k])
            elif stage == 2:
                for k in range(2):
                    add_into(gs.at[c, keep[k], u], r1s.at[slot, k])
            elif stage == 3:
                add_into(gs.at[c, home, u], r2s.at[slot])
        else:
            g = ge.at[place(u), c]
            if stage == 1:
                for k in range(4):
                    add_into(g.at[k], r0e.at[slot, k])
            elif stage == 2:
                for k in range(2):
                    add_into(g.at[keep[k]], r1e.at[slot, k])
            elif stage == 3:
                add_into(g.at[home], r2e.at[slot])
        if kind == "e" or stage < 3:
            start(kind, u, stage)

    def settle(kind, u):
        finish(kind, u, 3)
        if kind == "s":
            total = gs[c, home, zz].astype(f32)
            for i in range(nz - 1):
                total = total + r3s[i].astype(f32)
            os_[...] = total
            return
        total = ge[place(u), c, home, zz].astype(f32)
        for i in range(nz - 1):
            total = total + r3e[u, i].astype(f32)
        for h in range(2):
            half = total[24 * h : 24 * h + 24, :]
            if u < 4:
                oe[:, 768 * u + 384 * h : 768 * u + 384 * h + 384] = half
            elif u == 4:
                op[:, 384 * h : 384 * h + 384] = half
            else:
                for w in range(3):
                    at = 768 * w + 256 * (u - 5) + 128 * h
                    oq[:, at : at + 128] = half[:, 128 * w : 128 * w + 128]

    plan = {}
    for j in range(4):
        plan.setdefault(j + 1, []).extend([(1, "s", j), (1, "e", j)])
        plan.setdefault(j + 2, []).extend([(2, "s", j), (2, "e", j)])
        plan.setdefault(j + 3, []).extend([(3, "s", j), (3, "e", j)])
        plan.setdefault(j + 4, []).append((4, "e", j))
    plan.setdefault(7, []).append((5, "s", 0))
    plan.setdefault(9, []).append((6, "s", 0))
    for u, t in ((4, 4), (5, 6), (6, 8), (7, 10)):
        for stage in range(1, 5):
            plan.setdefault(t + stage, []).append((stage, "e", u))

    def tick(t, now=None):
        if not direct:
            return

        def act():
            for stage, kind, u in sorted(plan.get(t, []), key=lambda e: -e[0]):
                if stage == 6 or (stage == 4 and kind == "e"):
                    settle(kind, u)
                elif stage == 5:
                    start("s", 0, 3)
                else:
                    advance(kind, u, stage)

        if plan.get(t):
            if now is None:
                act()
            else:
                pl.when(now == t)(act)

    lane = lane_ids((BLK, 128))
    tiles = ROWS // BLK
    chunk = FF // 4

    def merge(own, other):
        def step(i, _):
            rows = pl.ds(pl.multiple_of(i * BLK, BLK), BLK)
            mine = row_ids((BLK, D)) + i * BLK >= a
            own[rows, :] = jnp.where(mine, own[rows, :].astype(f32), other[rows, :].astype(f32)).astype(bf16)
            return 0
        lax.fori_loop(0, SWAP // BLK, step, 0)

    def turn(src, dst, shift):
        def step(i, _):
            dst[pl.ds(pl.multiple_of(i * BLK, BLK), BLK), :] = rotated(src, shift, i).astype(bf16)
            return 0
        lax.fori_loop(0, tiles, step, 0)

    def expand_shares(slot, i, g):
        half = g.shape[1] // 2
        for n in range(16):
            part = g[24 * n : 24 * n + 24, :]
            part = jnp.concatenate([part[:, 0:half], part[:, half:]], axis=0).astype(bf16)
            yield (slot, n % 2, (n // 2) % 4, 2 * i + n // 8), part

    def front(we, ws, vt):
        loads = [load(src, dst, i) for i, (src, dst) in enumerate(
            ((tok_h, m), (wq_h, wq), (cot_h, n2), (wp_h, wp), (we_h, we), (ws_h, ws)))]
        for cp in loads[:4]:
            cp.start()
        swaps = [
            remote(src.at[pl.ds(0, SWAP)], dst, swap_send.at[i], swap_recv.at[i], partner)
            for i, (src, dst) in enumerate(((tok_h, tok_in), (cot_h, cot_in)))
        ]
        barrier = pltpu.get_barrier_semaphore()
        for f in friends:
            pl.semaphore_signal(barrier, inc=1, device_id=f, device_id_type=MESH)
        pl.semaphore_wait(barrier, len(friends))
        for cp in swaps:
            cp.start()
        for cp in loads[4:]:
            cp.start()
        vec[...] = jnp.zeros_like(vec)
        dn[...] = jnp.zeros_like(dn)
        loads[0].wait()
        swaps[0].wait()
        merge(m, tok_in)
        loads[1].wait()
        bound = jnp.where(c == 0, 0, ROWS - a)

        def project(i, _):
            r = pl.multiple_of(i * BLK, BLK)
            rows = pl.ds(r, BLK)
            xt = rotated(m, a, i)
            x[rows, :] = xt.astype(bf16)
            normed, _unused = row_stats(xt)
            nt_ = (normed * gain1[...].reshape(1, D) + shift1[...].reshape(1, D)).astype(bf16)
            n1[rows, :] = nt_
            qt = nn(nt_, wq[:, 0:D]) + qb[...].reshape(1, D)
            qt = (qt.astype(bf16).astype(f32) * 0.125).astype(bf16)
            q[rows, :] = qt
            qtt = qt.T
            k = nn(nt_, wq[:, D : 2 * D])
            vv = (nn(nt_, wq[:, 2 * D : 3 * D]) + vb[...].reshape(1, D)).astype(bf16)
            v[rows, :] = vv
            vt[:, rows] = vv.T
            k_flag = jnp.where(row_ids((BLK, 128)) + r >= bound, 0.0, masked_score).astype(f32)
            q_flag = jnp.where(lane_ids((1, BLK)) + r >= bound, 1.0, 0.0).astype(f32)
            q_spare = spare_rows(q_flag)
            for p in range(PAIRS):
                kp = k[:, 128 * p : 128 * p + 128]
                for s in range(2):
                    mine = lane < 64 if s == 0 else lane >= 64
                    base = 64 if s == 0 else 0
                    k_aug = jnp.where(lane == base, k_flag, 1.0)
                    k_aug = jnp.where(lane > base + 3, 0.0, k_aug)
                    at = 256 * p + 128 * s
                    kx[rows, at : at + 128] = jnp.where(mine, kp, k_aug).astype(bf16)
                    qxt[at : at + 128, rows] = with_spare(
                        s, qtt[128 * p + 64 * s : 128 * p + 64 * s + 64, :].astype(f32), q_spare)
            return 0

        lax.fori_loop(0, tiles, project, 0)
        triangle = row_ids((BLK, BLK)) <= lane_ids((BLK, BLK))
        jobs = [(i, s) for i in range(tiles) for s in range(2)]

        def attend(p, _):
            at = pl.multiple_of(p * 256, 256)
            pat = pl.multiple_of(p * 128, 128)

            def scores(i, s):
                qt = qxt[pl.ds(at + 128 * s, 128), BLK * i : BLK * i + BLK]
                st = [nn(kx[BLK * k : BLK * k + BLK, pl.ds(at + 128 * s, 128)], qt) for k in range(i + 1)]
                st[i] = jnp.where(triangle, st[i], masked_score)
                return st

            ready = [scores(*job) for job in jobs[:2]]
            for n, (i, s) in enumerate(jobs):
                st = ready.pop(0)
                if n + 2 < len(jobs):
                    ready.append(scores(*jobs[n + 2]))
                cols = slice(BLK * i, BLK * i + BLK)
                peak = jnp.max(st[0], axis=0, keepdims=True)
                for t in st[1:]:
                    peak = jnp.maximum(peak, jnp.max(t, axis=0, keepdims=True))
                vv = jnp.concatenate([vt[pl.ds(pat + 64 * s, 64), :], jnp.ones((16, ROWS), bf16)], axis=0)
                weights = [jnp.exp(t - peak).astype(bf16) for t in st]
                weights = weights[0] if i == 0 else jnp.concatenate(weights, axis=0)
                o = nn(vv[:, 0 : BLK * (i + 1)], weights)
                total = o[64:65, :]
                ctxt[pl.ds(pat + 64 * s, 64), cols] = (o[0:64, :] / total).astype(bf16)
                lse[pl.ds(2 * p + s, 1), cols] = peak + jnp.log(total)
            return 0

        lax.fori_loop(0, PAIRS, attend, 0)
        every = jnp.where(lane_ids((1, ROWS)) >= bound, 1.0, 0.0).astype(f32)
        for h in range(H):
            spare = spare_rows(every, *split3(-lse[h : h + 1, :]))
            at = 128 * h + (64 if h % 2 == 0 else 0)
            qxt[at : at + 64, :] = spare.astype(bf16)
        loads[2].wait()
        swaps[1].wait()
        merge(n2, cot_in)
        turn(n2, cot, a)
        loads[3].wait()

        def add_attended(i, _):
            rows = pl.ds(pl.multiple_of(i * BLK, BLK), BLK)
            mid = tn(ctxt[:, rows], wp[...]) + pb[...].reshape(1, D) + x[rows, :].astype(f32)
            acc[rows, :] = mid
            normed, _unused = row_stats(mid)
            n2[rows, :] = (normed * gain2[...].reshape(1, D) + shift2[...].reshape(1, D)).astype(bf16)
            return 0

        lax.fori_loop(0, tiles, add_attended, 0)
        save = load(acc, mid_h, 6)
        save.start()
        save.wait()
        loads[4].wait()
        loads[5].wait()

    def feed_forward(we, ws, low, grad):
        def one(j, _):
            cols = pl.ds(pl.multiple_of(j * chunk, chunk), chunk)

            def products(t):
                rows = slice(t * BLK, t * BLK + BLK)
                return (nn(n2[rows, :], we[:, cols]) + eb[cols].reshape(1, chunk),
                        nt(cot[rows, :], ws[cols, :]))

            bias_sum = jnp.zeros((1, chunk), f32)
            ready = products(0)
            for t in range(tiles):
                e, da = ready
                if t + 1 < tiles:
                    ready = products(t + 1)
                rows = slice(t * BLK, t * BLK + BLK)
                act, slope = gelu_parts(e)
                act = act.astype(bf16)
                de = (da * slope).astype(bf16)
                low[rows, :] = act
                grad[rows, :] = de
                acc[rows, :] += nn(act, ws[cols, :])
                dn[rows, :] += nt(de, we[:, cols])
                bias_sum = bias_sum + jnp.sum(de.astype(f32), axis=0, keepdims=True)
            vec[pl.ds(8 + j, 1), :] = bias_sum
            for t in range(1, 4):
                tick(t, j)
            for i in range(2):
                g = tn(low[:, 384 * i : 384 * i + 384], cot[...]).astype(bf16)
                for n in range(4):
                    gs[n % 2, 2 * i + n // 2, j] = g[96 * n : 96 * n + 96, :]
            start("s", j, 0)
            for i in range(2):
                for at, part in expand_shares(j, i, tn(n2[:, 384 * i : 384 * i + 384], grad[...])):
                    ge[at] = part
            start("e", j, 0)
            return 0

        lax.fori_loop(0, 4, one, 0)

    def first_half(we, ws):
        pl.run_scoped(functools.partial(front, we, ws), pltpu.VMEM((D, ROWS), bf16))
        pl.run_scoped(functools.partial(feed_forward, we, ws), pltpu.VMEM((ROWS, chunk), bf16), pltpu.VMEM((ROWS, chunk), bf16))

    pl.run_scoped(first_half, pltpu.VMEM((D, FF), bf16), pltpu.VMEM((FF, D), bf16))
    tick(4)

    out_give = [remote(cot.at[pl.ds(0, SWAP)], out_in_h, swap_send.at[2], swap_recv.at[2], partner),
                pltpu.make_async_copy(cot, out_h, out_sem.at[0])]
    ig_give = [remote(n2.at[pl.ds(0, SWAP)], ig_in_h, swap_send.at[3], swap_recv.at[3], partner),
               pltpu.make_async_copy(n2, ig_h, out_sem.at[1])]

    def middle(dot, do):
        def second(mid, ga_all):
            own = load(mid_h, mid, 6)
            own.start()
            own.wait()

            def tile(i, sums):
                r = pl.multiple_of(i * BLK, BLK)
                rows = pl.ds(r, BLK)
                m[rows, :] = (acc[rows, :] + sb[...].reshape(1, D)).astype(bf16)
                back, dgain, dshift = norm_back(mid[rows, :], gain2[...].reshape(1, D), dn[rows, :])
                ct = cot[rows, :].astype(f32)
                dmid = ct + back
                dn[rows, :] = dmid
                ga = dmid.astype(bf16)
                ga_all[rows, :] = ga
                dc = nt(ga, wp[...]).astype(bf16)
                do[rows, :] = dc
                dct = dc.T.astype(f32)
                prod = dct * ctxt[:, rows].astype(f32)
                for h in range(H):
                    inner = jnp.sum(prod[64 * h : 64 * h + 64, :], axis=0, keepdims=True)
                    dot[128 * h : 128 * h + 128, rows] = with_spare(
                        h % 2, dct[64 * h : 64 * h + 64, :], spare_rows(*split3(-inner)))
                dpb = jnp.sum(ga.astype(f32), axis=0, keepdims=True)
                dsb = jnp.sum(ct, axis=0, keepdims=True)
                return tuple(o + n for o, n in zip(sums, (dgain, dshift, dpb, dsb)))

            zero = jnp.zeros((1, D), f32)
            sums = lax.fori_loop(0, tiles, tile, (zero,) * 4)
            for at, s in zip((5, 6, 4, 7), sums):
                vec[at : at + 1, :] = s
            turn(m, cot, ROWS - a)
            for cp in out_give:
                cp.start()
            for i in range(2):
                for at, part in expand_shares(place(4), i, nn(ctxt[384 * i : 384 * i + 384, :], ga_all[...])):
                    ge[at] = part
            start("e", 4, 0)

        pl.run_scoped(second, pltpu.VMEM((ROWS, D), f32), pltpu.VMEM((ROWS, D), bf16))

    def attention(dot, do, dqkv):
        triangle = row_ids((BLK, BLK)) <= lane_ids((BLK, BLK))
        jobs = [(kb, qi, s) for kb in range(tiles) for qi in range(kb, tiles) for s in range(2)]

        def attention_loop(ktr, dqt):
            def pair(p, _):
                at = pl.multiple_of(p * 256, 256)
                pat = pl.multiple_of(p * 128, 128)
                pcols = pl.ds(pat, 128)
                lf = lane_ids((ROWS, 128))
                ktr[...] = jnp.where(lf < 64, kx[:, pl.ds(at, 128)], kx[:, pl.ds(at + 128, 128)]).T

                def scores(kb, qi, s):
                    krows = slice(BLK * kb, BLK * kb + BLK)
                    qrows = slice(BLK * qi, BLK * qi + BLK)
                    head = pl.ds(at + 128 * s, 128)
                    vd = v[krows, pcols]
                    vd = jnp.where(lane < 64 if s == 0 else lane >= 64, vd, jnp.ones_like(vd))
                    return nn(kx[krows, head], qxt[head, qrows]), nn(vd, dot[head, qrows])

                ready = [scores(*job) for job in jobs[:2]]
                dk, dv = {}, {}
                dv_sum = jnp.zeros((1, 128), f32)
                for n, (kb, qi, s) in enumerate(jobs):
                    st, dp = ready.pop(0)
                    if n + 2 < len(jobs):
                        ready.append(scores(*jobs[n + 2]))
                    krows = slice(BLK * kb, BLK * kb + BLK)
                    qrows = slice(BLK * qi, BLK * qi + BLK)
                    prob = jnp.exp(st)
                    if qi == kb:
                        prob = jnp.where(triangle, prob, 0.0)
                    ds = (prob * dp).astype(bf16)
                    dv_part = nn(prob.astype(bf16), do[qrows, pcols])
                    dk_part = nn(ds, q[qrows, pcols])
                    dv[s] = dv_part if qi == kb else dv[s] + dv_part
                    dk[s] = dk_part if qi == kb else dk[s] + dk_part
                    half = slice(64 * s, 64 * s + 64)
                    dq_part = nn(ktr[half, krows], ds)
                    if kb == 0:
                        dqt[half, qrows] = dq_part
                    else:
                        dqt[half, qrows] += dq_part
                    if s == 1 and qi == tiles - 1:
                        dqkv[krows, pl.ds(D + pat, 128)] = jnp.where(lane < 64, dk[0], dk[1]).astype(bf16)
                        dvp = jnp.where(lane < 64, dv[0], dv[1]).astype(bf16)
                        dqkv[krows, pl.ds(2 * D + pat, 128)] = dvp
                        dv_sum = dv_sum + jnp.sum(dvp.astype(f32), axis=0, keepdims=True)
                dq = (dqt[...] * 0.125).astype(bf16).T
                dqkv[:, pcols] = dq
                vec[2:3, pcols] = jnp.sum(dq.astype(f32), axis=0, keepdims=True)
                vec[3:4, pcols] = dv_sum
                for t in range(5, 11):
                    tick(t, p + 5)

                @pl.when(p % 2 == 1)
                def _():
                    k = p // 2
                    for i in range(2):
                        for w in range(3):
                            cols = pl.ds(pl.multiple_of(768 * w + 256 * k, 256), 256)
                            g = tn(n1[:, 384 * i : 384 * i + 384], dqkv[:, cols])
                            for at_, part in expand_shares(place(5 + k), i, g):
                                ge[at_ + (slice(None), slice(128 * w, 128 * w + 128))] = part
                    start("e", 5 + k, 0)

                return 0

            lax.fori_loop(0, PAIRS, pair, 0)

        pl.run_scoped(attention_loop, pltpu.VMEM((128, ROWS), bf16), pltpu.VMEM((128, ROWS), f32))

        def tile(i, sums):
            rows = pl.ds(pl.multiple_of(i * BLK, BLK), BLK)
            g = nt(dqkv[rows, :], wq[...])
            back, dgain, dshift = norm_back(x[rows, :].astype(f32), gain1[...].reshape(1, D), g)
            m[rows, :] = (dn[rows, :] + back).astype(bf16)
            for t in range(11, 15):
                tick(t, i + 11)
            return sums[0] + dgain, sums[1] + dshift

        zero = jnp.zeros((1, D), f32)
        sums = lax.fori_loop(0, tiles, tile, (zero,) * 2)
        vec[0:1, :] = sums[0]
        vec[1:2, :] = sums[1]
        turn(m, n2, ROWS - a)
        for cp in ig_give:
            cp.start()

    def second_half(dot, do):
        middle(dot, do)
        pl.run_scoped(functools.partial(attention, dot, do), pltpu.VMEM((ROWS, 3 * D), bf16))

    pl.run_scoped(second_half, pltpu.VMEM((2 * D, ROWS), bf16), pltpu.VMEM((ROWS, D), bf16))

    ends = list(out_give + ig_give)

    def emit(src, dst):
        cp = pltpu.make_async_copy(src, dst, out_sem.at[len(ends) - 2])
        cp.start()
        ends.append(cp)

    if direct:
        at = 0
        for group in ([partner], [xn], [yn], [(b % 4 + 4 * z, c) for z in zpeers]):
            cps = [remote(vec, vec_in.at[at + i], v_send.at[at + i], v_recv.at[at + i], to)
                   for i, to in enumerate(group)]
            for cp in cps:
                cp.start()
            for cp in cps:
                cp.wait()
            total = vec[...]
            for i in range(len(group)):
                total = total + vec_in[at + i]
            vec[...] = total
            at += len(group)
        emit(vec, vec_h)
        for src, dst in zip((oq, op, oe, os_), grads_h):
            emit(src, dst)
    else:
        emit(vec, vec_h)
        emit(gs, grads_h[0])
        emit(ge, grads_h[1])
    for cp in ends:
        cp.wait()


def layer_call(nz, direct, *args):
    unit = (48, 384)
    if direct:
        grads = [((24, 3 * D), f32), ((24, D), f32), ((24, FF), f32), ((96, D), f32)]
    else:
        grads = [((2, 4, 4, 96, D), bf16), ((8, 2, 4, 4) + unit, bf16)]
    shapes = [((ROWS, D), bf16), ((SWAP, D), bf16), ((ROWS, D), bf16), ((SWAP, D), bf16), ((16, D), f32),
              ((ROWS, D), f32)] + grads
    scratch = [
        pltpu.VMEM((2, 4, 4, 96, D), bf16), pltpu.VMEM((5 if direct else 8, 2, 4, 4) + unit, bf16),
        pltpu.VMEM((SWAP, D), bf16), pltpu.VMEM((SWAP, D), bf16),
        pltpu.VMEM((ROWS, D), bf16), pltpu.VMEM((ROWS, D), bf16),
        pltpu.VMEM((ROWS, D), bf16), pltpu.VMEM((ROWS, D), bf16),
        pltpu.VMEM((ROWS, D), bf16),
        pltpu.VMEM((2 * D, ROWS), bf16), pltpu.VMEM((ROWS, 2 * D), bf16),
        pltpu.VMEM((ROWS, D), bf16), pltpu.VMEM((D, ROWS), bf16),
        pltpu.VMEM((ROWS, D), f32), pltpu.VMEM((ROWS, D), f32),
        pltpu.VMEM((ROWS, D), bf16),
        pltpu.VMEM((D, 3 * D), bf16), pltpu.VMEM((D, D), bf16),
        pltpu.VMEM((16, ROWS), f32),
        pltpu.VMEM((16, D), f32), pltpu.VMEM((6, 16, D), f32),
        pltpu.SemaphoreType.DMA((7,)), pltpu.SemaphoreType.DMA((8,)),
        pltpu.SemaphoreType.DMA((4,)), pltpu.SemaphoreType.DMA((4,)),
    ]
    if direct:
        scratch += [
            pltpu.VMEM((2, 4, 96, D), bf16), pltpu.VMEM((2, 4, nz) + unit, bf16),
            pltpu.VMEM((2, 2, 96, D), bf16), pltpu.VMEM((2, 2, nz) + unit, bf16),
            pltpu.VMEM((2, 96, D), bf16), pltpu.VMEM((2, nz) + unit, bf16),
            pltpu.VMEM((nz - 1, 96, D), bf16), pltpu.VMEM((8, nz - 1) + unit, bf16),
            pltpu.VMEM((24, 3 * D), f32), pltpu.VMEM((24, D), f32), pltpu.VMEM((24, FF), f32), pltpu.VMEM((96, D), f32),
            pltpu.SemaphoreType.DMA((4, 4)), pltpu.SemaphoreType.DMA((4, 4)),
            pltpu.SemaphoreType.DMA((8, 7)), pltpu.SemaphoreType.DMA((8, 7)),
            pltpu.SemaphoreType.DMA((3,)), pltpu.SemaphoreType.DMA((3,)),
            pltpu.SemaphoreType.DMA((6,)), pltpu.SemaphoreType.DMA((6,)),
        ]
    return pl.pallas_call(
        functools.partial(layer_kernel, nz, direct),
        out_shape=[jax.ShapeDtypeStruct(s, t) for s, t in shapes],
        in_specs=[SMEM, ANY, ANY, VMEM, VMEM, ANY, VMEM, VMEM, ANY, VMEM, VMEM, VMEM, ANY, VMEM, ANY, VMEM],
        out_specs=[ANY] * len(shapes),
        scratch_shapes=scratch,
        compiler_params=pltpu.CompilerParams(
            collective_id=0, has_side_effects=True, vmem_limit_bytes=VMEM_LIMIT),
        cost_estimate=pl.CostEstimate(
            flops=64 * 10**9, bytes_accessed=40 * 10**6, transcendentals=20 * 10**6),
        name="layer",
    )(*args)


def swap_back_kernel(lens, out_own, out_in, ig_own, ig_in, out, ig):
    mine = row_ids((BLK, D)) + pl.program_id(0) * BLK >= lens[0, 0]
    out[...] = jnp.where(mine, out_own[...].astype(f32), out_in[...].astype(f32)).astype(bf16)
    ig[...] = jnp.where(mine, ig_own[...].astype(f32), ig_in[...].astype(f32))


def swap_back(lens, out_own, out_in, ig_own, ig_in):
    tile = pl.BlockSpec((BLK, D), lambda i: (i, 0))
    late = pl.BlockSpec((BLK, D), lambda i: (jnp.minimum(i, SWAP // BLK - 1), 0))
    return pl.pallas_call(
        swap_back_kernel,
        grid=(ROWS // BLK,),
        out_shape=[jax.ShapeDtypeStruct((ROWS, D), bf16), jax.ShapeDtypeStruct((ROWS, D), f32)],
        in_specs=[SMEM, tile, late, tile, late],
        out_specs=[tile, tile],
        cost_estimate=pl.CostEstimate(flops=10**6, bytes_accessed=10**7, transcendentals=0),
        name="swap_back",
    )(lens, out_own, out_in, ig_own, ig_in)


def on_device(nz, direct, tokens, lens, gain1, shift1, wq, qb, vb, wp, pb, gain2, shift2, we, eb, ws, sb, cot):
    out_own, out_in, ig_own, ig_in, vec, _mid, *grads = layer_call(
        nz, direct, lens, tokens, cot, gain1, shift1, wq, qb, vb, wp, pb, gain2, shift2, we, eb, ws, sb)
    out, ig = swap_back(lens, out_own, out_in, ig_own, ig_in)
    shards = lax.axis_size("batch") * 2
    me = lax.axis_index("batch") * 2 + lax.axis_index("seq")

    if direct:
        gq, gp, ge, gs = grads

        def own_part(row, rows=1):
            flat = vec[row : row + rows].reshape(rows * D)
            n = rows * D // shards
            return lax.dynamic_slice(flat, (me * n,), (n,))
    else:
        def scatter(g):
            return lax.psum_scatter(g, ("batch", "seq"), scatter_dimension=0, tiled=True)

        def own_part(row, rows=1):
            return scatter(vec[row : row + rows].reshape(rows * D))

        us, ue = (g.astype(f32) for g in grads)
        gs = scatter(us.transpose(2, 1, 0, 3, 4).reshape(FF, D))
        ue = ue.reshape(8, 2, 4, 4, 2, 24, 384)
        wide = ue[:5].transpose(3, 2, 1, 5, 0, 4, 6).reshape(D, 5 * D)
        ge = scatter(wide[:, :FF])
        gp = scatter(wide[:, FF:])
        gq = ue[5:].reshape(3, 2, 4, 4, 2, 24, 3, 128).transpose(3, 2, 1, 5, 6, 0, 4, 7).reshape(D, 3 * D)
        gq = scatter(gq)
    return (out, ig, own_part(0), own_part(1), gq, own_part(2), own_part(3), gp, own_part(4),
            own_part(5), own_part(6), ge, own_part(8, 4), gs, own_part(7))


def solution(mesh):
    nz = mesh.shape["batch"] // 4
    direct = mesh.shape["batch"] == 16 and mesh.shape["seq"] == 2
    rows = P(("batch", "seq"), None)
    part = P(("batch", "seq"))
    whole = P()
    in_specs = (rows, P("batch", None)) + (whole,) * 13 + (rows,)
    out_specs = (rows, rows, part, part, rows, part, part, rows, part, part, part, rows, part, rows, part)
    return jax.shard_map(
        functools.partial(on_device, nz, direct),
        mesh=mesh, in_specs=in_specs, out_specs=out_specs, check_vma=False)
```

time: 225 us -> 183 us (0.81)
  Pallas kernels: 212 us -> 176 us
  local copies, waits for them, and re-layouts: 12.1 us -> 5.74 us
    pallas_call x2, Pallas kernels: 212 us -> 176 us  [the longest x1 171 us: layer_call(): pl.pallas_call(functools.partial(layer_kernel, nz, direct), out_shape=[ja...]
    unnamed x16 -> x14, local copies, waits for them, and re-layouts: 7.23 us -> 2.77 us
where the time goes in v2:
time: 183 us
  Pallas kernels  176 us (96%)
  local copies, waits for them, and re-layouts  5.74 us (3%)
    pallas_call x1, Pallas kernels, layer_call(): pl.pallas_call(functools.partial(layer_kernel, nz, direct), out_shape=[ja...  171 us
    pallas_call x1, Pallas kernels, swap_back(): pl.pallas_call(swap_back_kernel, grid=(ROWS // BLK,), out_shape=[jax.Shap...  5.39 us

profile of v2, /device:TPU:0, one launch (start us, length us, event | category | flops | bytes accessed | tf_op | source)
XLA Modules:
  0.0 182.8 jit_solution(9696132630184635890)
XLA Ops:
  0.7 171.0 %layer.1 = (bf16[1024,768]{1,0:T(8,128)(2,1)}, bf16[768,768]{1,0:T(8,128)(2,1)}, bf16[1024,768]{1,0:T(8,128)(2,1)}, bf16[768,768]{1,0:T(8,128)(2,1)}, f32[16,768...) custom-call(s32[1,3]{1,0:T(1,128)} %lens.3, ...), custom_call_target="tpu_custom_call" | custom-call | flops 64000000000 | bytes 40000000 | tf_op jit(solution)/shard_map/layer/pallas_call | solution.py:661
  171.7 0.0 copy-start.4
  171.7 0.0 copy-start.2
  171.7 0.0 copy-start.3
  171.7 0.0 copy-start.1
  171.7 0.0 copy-start
  171.7 5.4 %swap_back.1 = (bf16[1024,768]{1,0:T(8,128)(2,1)}, f32[1024,768]{1,0:T(8,128)}) custom-call(s32[1,3]{1,0:T(1,128)} %lens.3, bf16[1024,768]{1,0:T(8,128)(2,1)} %get-tuple-element.26.out_own, bf16[768,768]{1,0:T(8,128)(2,1)} %get-tuple-element.27.out_in, bf16[1024,768]{1,0:T(8,128)(2,1)} %get-tuple-element.28.ig_own, bf16[768,768]{1,0:T(8,128)(2,1)} %get-tuple-element.29.ig_in), custom_call_target="tpu_custom_call" | custom-call | flops 1000000 | bytes 10000000 | tf_op jit(solution)/shard_map/swap_back/pallas_call | solution.py:684
  177.1 0.0 copy-done.4
  177.1 0.6 fusion
  177.7 0.6 fusion.2
  178.3 0.6 fusion.4
  178.9 0.6 fusion.6
  179.5 0.6 dynamic_slice.57
  180.1 0.0 copy-done.2
  180.1 0.7 copy.35
  180.8 0.0 copy-done.3
  180.8 0.6 copy.36
  181.4 0.0 copy-done.1
  181.4 0.7 copy.37
  182.1 0.0 copy-done
  182.1 0.7 copy.38
  (3 shorter events, 0.0 us)
Async XLA Ops:
  171.7 5.4 %copy-start.4 = (f32[16,768]{1,0:T(8,128)S(1)}, f32[16,768]{1,0:T(8,128)}, u32[]{:S(2)}) copy-start(f32[16,768]{1,0:T(8,128)} %get-tuple-element.32) | copy-start | bytes 147460
  171.7 8.4 %copy-start.2 = (f32[24,2304]{1,0:T(8,128)S(1)}, f32[24,2304]{1,0:T(8,128)}, u32[]{:S(2)}) copy-start(f32[24,2304]{1,0:T(8,128)} %get-tuple-element.72) | copy-start | bytes 663556
  171.7 9.1 %copy-start.3 = (f32[24,768]{1,0:T(8,128)S(1)}, f32[24,768]{1,0:T(8,128)}, u32[]{:S(2)}) copy-start(f32[24,768]{1,0:T(8,128)} %get-tuple-element.75) | copy-start | bytes 221188
  171.7 9.7 %copy-start.1 = (f32[24,3072]{1,0:T(8,128)S(1)}, f32[24,3072]{1,0:T(8,128)}, u32[]{:S(2)}) copy-start(f32[24,3072]{1,0:T(8,128)} %get-tuple-element.79) | copy-start | bytes 884740
  171.7 10.4 %copy-start = (f32[96,768]{1,0:T(8,128)S(1)}, f32[96,768]{1,0:T(8,128)}, u32[]{:S(2)}) copy-start(f32[96,768]{1,0:T(8,128)} %get-tuple-element.81) | copy-start | bytes 884740

commit v3 on v2

--- a/solution.py
+++ b/solution.py
@@ -24,7 +24,7 @@
 FF = 3072
 PAIRS = 6
 BLK = 256
-VMEM_LIMIT = 63 * 2**20
+VMEM_LIMIT = 65000 * 2**10
 GELU_C = 0.7978845608028654
 
 
@@ -123,8 +123,6 @@
     yy = (b // 2) % 2
     zz = b // 4
     partner = (b, 1 - c)
-    xn = (b + 1 - 2 * xx, c)
-    yn = (b + 2 - 4 * yy, c)
     n1st = (b + (1 - c) * (1 - 2 * xx) + c * (2 - 4 * yy), c)
     n2nd = (b + c * (1 - 2 * xx) + (1 - c) * (2 - 4 * yy), c)
     zpeers = [(zz + i) % nz for i in range(1, nz)] if direct else []
@@ -134,7 +132,8 @@
     home = 2 * yy + xx
     friends = [partner]
     if direct:
-        friends += [xn, yn] + [(b % 4 + 4 * z, c) for z in zpeers]
+        cube = [(b - b % 4 + (yy + n // 2) % 2 * 2 + (xx + n) % 2, (c + n // 4) % 2) for n in range(1, 8)]
+        friends = cube + [(b % 4 + 4 * z, c) for z in zpeers]
 
     def load(src, dst, i):
         return pltpu.make_async_copy(src, dst, load_sem.at[i])
@@ -153,21 +152,21 @@
             if stage == 0:
                 return [remote(gs.at[1 - c, :, u], r0s.at[slot], s_send.at[u, 0], s_recv.at[u, 0], partner)]
             if stage == 1:
-                return [remote(gs.at[c, give[k], u], r1s.at[slot, k], s_send.at[u, 1 + k], s_recv.at[u, 1 + k], n1st)
+                return [remote(gs.at[c, give[k], u], r1s.at[u % 4, k], s_send.at[u, 1 + k], s_recv.at[u, 1 + k], n1st)
                         for k in range(2)]
             if stage == 2:
-                return [remote(gs.at[c, give2, u], r2s.at[slot], s_send.at[u, 3], s_recv.at[u, 3], n2nd)]
+                return [remote(gs.at[c, give2, u], r2s.at[u % 4], s_send.at[u, 3], s_recv.at[u, 3], n2nd)]
             return [remote(gs.at[c, home, z], r3s.at[i], j_send.at[i], j_recv.at[i], (b % 4 + 4 * z, c))
                     for i, z in enumerate(zpeers)]
         g = ge.at[place(u)]
         if stage == 0:
             return [remote(g.at[1 - c], r0e.at[slot], e_send.at[u, 0], e_recv.at[u, 0], partner)]
         if stage == 1:
-            return [remote(g.at[c, give[k]], r1e.at[slot, k], e_send.at[u, 1 + k], e_recv.at[u, 1 + k], n1st)
+            return [remote(g.at[c, give[k]], r1e.at[u % 4, k], e_send.at[u, 1 + k], e_recv.at[u, 1 + k], n1st)
                     for k in range(2)]
         if stage == 2:
-            return [remote(g.at[c, give2], r2e.at[slot], e_send.at[u, 3], e_recv.at[u, 3], n2nd)]
-        return [remote(g.at[c, home, z], r3e.at[u, i], e_send.at[u, 4 + i], e_recv.at[u, 4 + i],
+            return [remote(g.at[c, give2], r2e.at[u % 4], e_send.at[u, 3], e_recv.at[u, 3], n2nd)]
+        return [remote(g.at[c, home, z], r3e.at[u % 4, i], e_send.at[u, 4 + i], e_recv.at[u, 4 + i],
                        (b % 4 + 4 * z, c)) for i, z in enumerate(zpeers)]
 
     def start(kind, u, stage):
@@ -180,7 +179,7 @@
             cp.wait()
 
     def add_into(dst, src):
-        dst[...] = (dst[...].astype(f32) + src[...].astype(f32)).astype(bf16)
+        dst[...] = dst[...] + src[...]
 
     def advance(kind, u, stage):
         finish(kind, u, stage - 1)
@@ -191,9 +190,9 @@
                     add_into(gs.at[c, k, u], r0s.at[slot, k])
             elif stage == 2:
                 for k in range(2):
-                    add_into(gs.at[c, keep[k], u], r1s.at[slot, k])
+                    add_into(gs.at[c, keep[k], u], r1s.at[u % 4, k])
             elif stage == 3:
-                add_into(gs.at[c, home, u], r2s.at[slot])
+                add_into(gs.at[c, home, u], r2s.at[u % 4])
         else:
             g = ge.at[place(u), c]
             if stage == 1:
@@ -201,9 +200,9 @@
                     add_into(g.at[k], r0e.at[slot, k])
             elif stage == 2:
                 for k in range(2):
-                    add_into(g.at[keep[k]], r1e.at[slot, k])
+                    add_into(g.at[keep[k]], r1e.at[u % 4, k])
             elif stage == 3:
-                add_into(g.at[home], r2e.at[slot])
+                add_into(g.at[home], r2e.at[u % 4])
         if kind == "e" or stage < 3:
             start(kind, u, stage)
 
@@ -217,7 +216,7 @@
             return
         total = ge[place(u), c, home, zz].astype(f32)
         for i in range(nz - 1):
-            total = total + r3e[u, i].astype(f32)
+            total = total + r3e[u % 4, i].astype(f32)
         for h in range(2):
             half = total[24 * h : 24 * h + 24, :]
             if u < 4:
@@ -229,36 +228,23 @@
                     at = 768 * w + 256 * (u - 5) + 128 * h
                     oq[:, at : at + 128] = half[:, 128 * w : 128 * w + 128]
 
-    plan = {}
-    for j in range(4):
-        plan.setdefault(j + 1, []).extend([(1, "s", j), (1, "e", j)])
-        plan.setdefault(j + 2, []).extend([(2, "s", j), (2, "e", j)])
-        plan.setdefault(j + 3, []).extend([(3, "s", j), (3, "e", j)])
-        plan.setdefault(j + 4, []).append((4, "e", j))
-    plan.setdefault(7, []).append((5, "s", 0))
-    plan.setdefault(9, []).append((6, "s", 0))
-    for u, t in ((4, 4), (5, 6), (6, 8), (7, 10)):
-        for stage in range(1, 5):
-            plan.setdefault(t + stage, []).append((stage, "e", u))
-
-    def tick(t, now=None):
+    def steps(todo, when=None):
         if not direct:
             return
 
         def act():
-            for stage, kind, u in sorted(plan.get(t, []), key=lambda e: -e[0]):
-                if stage == 6 or (stage == 4 and kind == "e"):
+            for kind, u, stage in todo:
+                if stage == 4:
                     settle(kind, u)
-                elif stage == 5:
-                    start("s", 0, 3)
+                elif stage == "join":
+                    start(kind, u, 3)
                 else:
                     advance(kind, u, stage)
 
-        if plan.get(t):
-            if now is None:
-                act()
-            else:
-                pl.when(now == t)(act)
+        if when is None:
+            act()
+        else:
+            pl.when(when)(act)
 
     lane = lane_ids((BLK, 128))
     tiles = ROWS // BLK
@@ -392,16 +378,17 @@
             acc[rows, :] = mid
             normed, _unused = row_stats(mid)
             n2[rows, :] = (normed * gain2[...].reshape(1, D) + shift2[...].reshape(1, D)).astype(bf16)
+            pltpu.make_async_copy(acc.at[rows], mid_h.at[rows], load_sem.at[6]).start()
             return 0
 
         lax.fori_loop(0, tiles, add_attended, 0)
-        save = load(acc, mid_h, 6)
-        save.start()
-        save.wait()
+        load(acc, mid_h, 6).wait()
         loads[4].wait()
         loads[5].wait()
 
-    def feed_forward(we, ws, low, grad):
+    def feed_forward(we, ws, grad):
+        low = m
+
         def one(j, _):
             cols = pl.ds(pl.multiple_of(j * chunk, chunk), chunk)
 
@@ -425,9 +412,15 @@
                 acc[rows, :] += nn(act, ws[cols, :])
                 dn[rows, :] += nt(de, we[:, cols])
                 bias_sum = bias_sum + jnp.sum(de.astype(f32), axis=0, keepdims=True)
+                if t == 0:
+                    steps([("s", j - 2, 2)], j >= 2)
+                elif t == 1:
+                    steps([("s", j - 1, 1)], j >= 1)
+                elif t == 2:
+                    steps([("e", j - 3, 2)], j >= 3)
+                else:
+                    steps([("e", j - 1, 1)], j >= 1)
             vec[pl.ds(8 + j, 1), :] = bias_sum
-            for t in range(1, 4):
-                tick(t, j)
             for i in range(2):
                 g = tn(low[:, 384 * i : 384 * i + 384], cot[...]).astype(bf16)
                 for n in range(4):
@@ -443,10 +436,21 @@
 
     def first_half(we, ws):
         pl.run_scoped(functools.partial(front, we, ws), pltpu.VMEM((D, ROWS), bf16))
-        pl.run_scoped(functools.partial(feed_forward, we, ws), pltpu.VMEM((ROWS, chunk), bf16), pltpu.VMEM((ROWS, chunk), bf16))
+        pl.run_scoped(functools.partial(feed_forward, we, ws), pltpu.VMEM((ROWS, chunk), bf16))
 
     pl.run_scoped(first_half, pltpu.VMEM((D, FF), bf16), pltpu.VMEM((FF, D), bf16))
-    tick(4)
+    def total_copies(n):
+        to = cube if n == 0 else [(b % 4 + 4 * z, c) for z in zpeers]
+        at = 7 * n
+        return [remote(vec, vec_in.at[at + i], v_send.at[at + i], v_recv.at[at + i], t) for i, t in enumerate(to)]
+
+    def total_hop(n):
+        for cp in total_copies(n):
+            cp.wait()
+        total = vec[...]
+        for i in range(len(total_copies(n))):
+            total = total + vec_in[7 * n + i]
+        vec[...] = total
 
     out_give = [remote(cot.at[pl.ds(0, SWAP)], out_in_h, swap_send.at[2], swap_recv.at[2], partner),
                 pltpu.make_async_copy(cot, out_h, out_sem.at[0])]
@@ -460,8 +464,7 @@
             own.wait()
 
             def tile(i, sums):
-                r = pl.multiple_of(i * BLK, BLK)
-                rows = pl.ds(r, BLK)
+                rows = slice(i * BLK, i * BLK + BLK)
                 m[rows, :] = (acc[rows, :] + sb[...].reshape(1, D)).astype(bf16)
                 back, dgain, dshift = norm_back(mid[rows, :], gain2[...].reshape(1, D), dn[rows, :])
                 ct = cot[rows, :].astype(f32)
@@ -477,12 +480,18 @@
                     inner = jnp.sum(prod[64 * h : 64 * h + 64, :], axis=0, keepdims=True)
                     dot[128 * h : 128 * h + 128, rows] = with_spare(
                         h % 2, dct[64 * h : 64 * h + 64, :], spare_rows(*split3(-inner)))
+                for n, todo in enumerate((
+                    [("s", 3, 1)], [("e", 3, 1)], [("e", 1, 2)], [("s", 2, 2)])):
+                    if i == n:
+                        steps(todo)
                 dpb = jnp.sum(ga.astype(f32), axis=0, keepdims=True)
                 dsb = jnp.sum(ct, axis=0, keepdims=True)
                 return tuple(o + n for o, n in zip(sums, (dgain, dshift, dpb, dsb)))
 
             zero = jnp.zeros((1, D), f32)
-            sums = lax.fori_loop(0, tiles, tile, (zero,) * 4)
+            sums = (zero,) * 4
+            for i in range(tiles):
+                sums = tile(i, sums)
             for at, s in zip((5, 6, 4, 7), sums):
                 vec[at : at + 1, :] = s
             turn(m, cot, ROWS - a)
@@ -538,6 +547,15 @@
                         dqt[half, qrows] = dq_part
                     else:
                         dqt[half, qrows] += dq_part
+                    if n == len(jobs) // 2:
+                        for r, todo in enumerate((
+                            [("s", 0, 3), ("e", 0, 3), ("s", 1, 3), ("e", 2, 2), ("e", 4, 1)],
+                            [("e", 0, 4), ("e", 1, 3), ("s", 3, 2), ("e", 3, 2)],
+                            [("s", 2, 3), ("e", 2, 3), ("e", 4, 2), ("e", 5, 1)],
+                            [("e", 1, 4), ("s", 3, 3), ("e", 3, 3)],
+                            [("e", 2, 4), ("s", 0, "join"), ("e", 4, 3), ("e", 5, 2), ("e", 6, 1)],
+                            [("e", 3, 4)])):
+                            steps(todo, p == r)
                     if s == 1 and qi == tiles - 1:
                         dqkv[krows, pl.ds(D + pat, 128)] = jnp.where(lane < 64, dk[0], dk[1]).astype(bf16)
                         dvp = jnp.where(lane < 64, dv[0], dv[1]).astype(bf16)
@@ -547,9 +565,6 @@
                 dqkv[:, pcols] = dq
                 vec[2:3, pcols] = jnp.sum(dq.astype(f32), axis=0, keepdims=True)
                 vec[3:4, pcols] = dv_sum
-                for t in range(5, 11):
-                    tick(t, p + 5)
-
                 @pl.when(p % 2 == 1)
                 def _():
                     k = p // 2
@@ -572,14 +587,18 @@
             g = nt(dqkv[rows, :], wq[...])
             back, dgain, dshift = norm_back(x[rows, :].astype(f32), gain1[...].reshape(1, D), g)
             m[rows, :] = (dn[rows, :] + back).astype(bf16)
-            for t in range(11, 15):
-                tick(t, i + 11)
+            for n, todo in enumerate((
+                [("e", 4, 4), ("e", 5, 3), ("e", 6, 2), ("e", 7, 1)], [("s", 0, 4)], [], [("e", 7, 2)])):
+                steps(todo, i == n)
             return sums[0] + dgain, sums[1] + dshift
 
         zero = jnp.zeros((1, D), f32)
         sums = lax.fori_loop(0, tiles, tile, (zero,) * 2)
         vec[0:1, :] = sums[0]
         vec[1:2, :] = sums[1]
+        if direct:
+            for cp in total_copies(0):
+                cp.start()
         turn(m, n2, ROWS - a)
         for cp in ig_give:
             cp.start()
@@ -598,19 +617,12 @@
         ends.append(cp)
 
     if direct:
-        at = 0
-        for group in ([partner], [xn], [yn], [(b % 4 + 4 * z, c) for z in zpeers]):
-            cps = [remote(vec, vec_in.at[at + i], v_send.at[at + i], v_recv.at[at + i], to)
-                   for i, to in enumerate(group)]
-            for cp in cps:
-                cp.start()
-            for cp in cps:
-                cp.wait()
-            total = vec[...]
-            for i in range(len(group)):
-                total = total + vec_in[at + i]
-            vec[...] = total
-            at += len(group)
+        steps([("e", 5, 4), ("e", 6, 3), ("e", 7, 3)])
+        total_hop(0)
+        for cp in total_copies(1):
+            cp.start()
+        steps([("e", 6, 4), ("e", 7, 4)])
+        total_hop(1)
         emit(vec, vec_h)
         for src, dst in zip((oq, op, oe, os_), grads_h):
             emit(src, dst)
@@ -642,21 +654,21 @@
         pltpu.VMEM((ROWS, D), bf16),
         pltpu.VMEM((D, 3 * D), bf16), pltpu.VMEM((D, D), bf16),
         pltpu.VMEM((16, ROWS), f32),
-        pltpu.VMEM((16, D), f32), pltpu.VMEM((6, 16, D), f32),
+        pltpu.VMEM((16, D), f32), pltpu.VMEM((10 if direct else 1, 16, D), f32),
         pltpu.SemaphoreType.DMA((7,)), pltpu.SemaphoreType.DMA((8,)),
         pltpu.SemaphoreType.DMA((4,)), pltpu.SemaphoreType.DMA((4,)),
     ]
     if direct:
         scratch += [
             pltpu.VMEM((2, 4, 96, D), bf16), pltpu.VMEM((2, 4, nz) + unit, bf16),
-            pltpu.VMEM((2, 2, 96, D), bf16), pltpu.VMEM((2, 2, nz) + unit, bf16),
-            pltpu.VMEM((2, 96, D), bf16), pltpu.VMEM((2, nz) + unit, bf16),
-            pltpu.VMEM((nz - 1, 96, D), bf16), pltpu.VMEM((8, nz - 1) + unit, bf16),
+            pltpu.VMEM((4, 2, 96, D), bf16), pltpu.VMEM((4, 2, nz) + unit, bf16),
+            pltpu.VMEM((4, 96, D), bf16), pltpu.VMEM((4, nz) + unit, bf16),
+            pltpu.VMEM((nz - 1, 96, D), bf16), pltpu.VMEM((4, nz - 1) + unit, bf16),
             pltpu.VMEM((24, 3 * D), f32), pltpu.VMEM((24, D), f32), pltpu.VMEM((24, FF), f32), pltpu.VMEM((96, D), f32),
             pltpu.SemaphoreType.DMA((4, 4)), pltpu.SemaphoreType.DMA((4, 4)),
             pltpu.SemaphoreType.DMA((8, 7)), pltpu.SemaphoreType.DMA((8, 7)),
             pltpu.SemaphoreType.DMA((3,)), pltpu.SemaphoreType.DMA((3,)),
-            pltpu.SemaphoreType.DMA((6,)), pltpu.SemaphoreType.DMA((6,)),
+            pltpu.SemaphoreType.DMA((10,)), pltpu.SemaphoreType.DMA((10,)),
         ]
     return pl.pallas_call(
         functools.partial(layer_kernel, nz, direct),
@@ -672,47 +684,98 @@
     )(*args)
 
 
-def swap_back_kernel(lens, out_own, out_in, ig_own, ig_in, out, ig):
-    mine = row_ids((BLK, D)) + pl.program_id(0) * BLK >= lens[0, 0]
-    out[...] = jnp.where(mine, out_own[...].astype(f32), out_in[...].astype(f32)).astype(bf16)
-    ig[...] = jnp.where(mine, ig_own[...].astype(f32), ig_in[...].astype(f32))
-
-
-def swap_back(lens, out_own, out_in, ig_own, ig_in):
-    tile = pl.BlockSpec((BLK, D), lambda i: (i, 0))
-    late = pl.BlockSpec((BLK, D), lambda i: (jnp.minimum(i, SWAP // BLK - 1), 0))
+def final_kernel(
+    direct, shards, lens, out_own, out_in, ig_own, ig_in, vec, *rest,
+):
+    moved = 4 if direct else 0
+    given = 9 if direct else 0
+    grads = rest[:moved]
+    out, ig = rest[moved : moved + 2]
+    grads_to = rest[moved + 2 : 2 * moved + 2]
+    parts = rest[2 * moved + 2 : 2 * moved + 2 + given]
+    own, inn, igo, igi, res, load_sem, save_sem = rest[2 * moved + 2 + given :]
+    a = lens[0, 0]
+    tiles = ROWS // BLK
+    loads = []
+    for t in range(tiles):
+        rows = pl.ds(t * BLK, BLK)
+        some = [(ig_own, igo), (out_own, own)]
+        if t * BLK < SWAP:
+            some += [(ig_in, igi), (out_in, inn)]
+        loads.append([pltpu.make_async_copy(src.at[rows], dst.at[rows], load_sem.at[t, i])
+                      for i, (src, dst) in enumerate(some)])
+    for group in loads:
+        for cp in group:
+            cp.start()
+    for src, dst in zip(grads, grads_to):
+        dst[...] = src[...]
+    if direct:
+        me = lax.axis_index("batch") * 2 + lax.axis_index("seq")
+
+        def columns(v, first, n):
+            shape = (D, 128)
+            pick = (row_ids(shape) == lane_ids(shape) + first) & (lane_ids(shape) < n)
+            return jnp.dot(v, pick.astype(f32), precision=lax.Precision.HIGHEST, preferred_element_type=f32)
+
+        n = D // shards
+        narrow = columns(vec[...], n * me, n)
+        for i in range(8):
+            parts[i][...] = narrow[i, :n]
+        n = FF // shards
+        wide = columns(vec[8:12, :], n * (me % (D // n)), n)
+        wide = jnp.sum(jnp.where(row_ids(wide.shape) == me // (D // n), wide, 0.0), axis=0)
+        parts[8][...] = wide[:n]
+    saves = []
+    for t in range(tiles):
+        for cp in loads[t]:
+            cp.wait()
+        rows = slice(t * BLK, t * BLK + BLK)
+        g = igo[rows, :].astype(f32)
+        if t * BLK < SWAP:
+            mine = row_ids((BLK, D)) + t * BLK >= a
+            own[rows, :] = jnp.where(mine, own[rows, :].astype(f32), inn[rows, :].astype(f32)).astype(bf16)
+            g = jnp.where(mine, g, igi[rows, :].astype(f32))
+        res[rows, :] = g
+        for i, (src, dst) in enumerate(((own, out), (res, ig))):
+            saves.append(pltpu.make_async_copy(src.at[pl.ds(t * BLK, BLK)], dst.at[pl.ds(t * BLK, BLK)], save_sem.at[t, i]))
+            saves[-1].start()
+    for cp in saves:
+        cp.wait()
+
+
+def final_call(direct, shards, lens, out_own, out_in, ig_own, ig_in, vec, *grads):
+    tiles = ROWS // BLK
+    parts = [D // shards] * 8 + [FF // shards] if direct else []
     return pl.pallas_call(
-        swap_back_kernel,
-        grid=(ROWS // BLK,),
-        out_shape=[jax.ShapeDtypeStruct((ROWS, D), bf16), jax.ShapeDtypeStruct((ROWS, D), f32)],
-        in_specs=[SMEM, tile, late, tile, late],
-        out_specs=[tile, tile],
-        cost_estimate=pl.CostEstimate(flops=10**6, bytes_accessed=10**7, transcendentals=0),
-        name="swap_back",
-    )(lens, out_own, out_in, ig_own, ig_in)
+        functools.partial(final_kernel, direct, shards),
+        out_shape=[jax.ShapeDtypeStruct((ROWS, D), bf16), jax.ShapeDtypeStruct((ROWS, D), f32)]
+        + [jax.ShapeDtypeStruct(g.shape, g.dtype) for g in grads] + [jax.ShapeDtypeStruct((n,), f32) for n in parts],
+        in_specs=[SMEM] + [ANY] * 4 + [VMEM] * (1 + len(grads)),
+        out_specs=[ANY] * 2 + [VMEM] * (len(grads) + len(parts)),
+        scratch_shapes=[
+            pltpu.VMEM((ROWS, D), bf16), pltpu.VMEM((SWAP, D), bf16), pltpu.VMEM((ROWS, D), bf16),
+            pltpu.VMEM((SWAP, D), bf16), pltpu.VMEM((ROWS, D), f32),
+            pltpu.SemaphoreType.DMA((tiles, 4)), pltpu.SemaphoreType.DMA((tiles, 2)),
+        ],
+        compiler_params=pltpu.CompilerParams(vmem_limit_bytes=VMEM_LIMIT),
+        cost_estimate=pl.CostEstimate(flops=10**6, bytes_accessed=12 * 10**6, transcendentals=0),
+        name="final",
+    )(lens, out_own, out_in, ig_own, ig_in, vec, *grads)
 
 
 def on_device(nz, direct, tokens, lens, gain1, shift1, wq, qb, vb, wp, pb, gain2, shift2, we, eb, ws, sb, cot):
     out_own, out_in, ig_own, ig_in, vec, _mid, *grads = layer_call(
         nz, direct, lens, tokens, cot, gain1, shift1, wq, qb, vb, wp, pb, gain2, shift2, we, eb, ws, sb)
-    out, ig = swap_back(lens, out_own, out_in, ig_own, ig_in)
     shards = lax.axis_size("batch") * 2
-    me = lax.axis_index("batch") * 2 + lax.axis_index("seq")
-
+    out, ig, *rest = final_call(direct, shards, lens, out_own, out_in, ig_own, ig_in, vec, *(grads if direct else ()))
     if direct:
-        gq, gp, ge, gs = grads
-
-        def own_part(row, rows=1):
-            flat = vec[row : row + rows].reshape(rows * D)
-            n = rows * D // shards
-            return lax.dynamic_slice(flat, (me * n,), (n,))
+        gq, gp, ge, gs = rest[:4]
+        parts = rest[4:]
     else:
         def scatter(g):
             return lax.psum_scatter(g, ("batch", "seq"), scatter_dimension=0, tiled=True)
 
-        def own_part(row, rows=1):
-            return scatter(vec[row : row + rows].reshape(rows * D))
-
+        parts = [scatter(vec[i]) for i in range(8)] + [scatter(vec[8:12].reshape(FF))]
         us, ue = (g.astype(f32) for g in grads)
         gs = scatter(us.transpose(2, 1, 0, 3, 4).reshape(FF, D))
         ue = ue.reshape(8, 2, 4, 4, 2, 24, 384)
@@ -721,8 +784,8 @@
         gp = scatter(wide[:, FF:])
         gq = ue[5:].reshape(3, 2, 4, 4, 2, 24, 3, 128).transpose(3, 2, 1, 5, 6, 0, 4, 7).reshape(D, 3 * D)
         gq = scatter(gq)
-    return (out, ig, own_part(0), own_part(1), gq, own_part(2), own_part(3), gp, own_part(4),
-            own_part(5), own_part(6), ge, own_part(8, 4), gs, own_part(7))
+    return (out, ig, parts[0], parts[1], gq, parts[2], parts[3], gp, parts[4],
+            parts[5], parts[6], ge, parts[8], gs, parts[7])
 
 
 def solution(mesh):

time: 183 us -> 151 us (0.83)
  Pallas kernels: 176 us -> 150 us
  local copies, waits for them, and re-layouts: 5.74 us -> 0 us
    pallas_call x1, Pallas kernels: 171 us -> 143 us  [layer_call(): pl.pallas_call(functools.partial(layer_kernel, nz, direct), out_shape=[ja...]
    dynamic_slice x5 -> x0, local copies, waits for them, and re-layouts: 2.94 us -> none  [own_part(): return lax.dynamic_slice(flat, (me * n,), (n,))]
    unnamed x14 -> x0, local copies, waits for them, and re-layouts: 2.77 us -> none
where the time goes in v3:
time: 151 us
  Pallas kernels  150 us (99%)
    pallas_call x1, Pallas kernels, layer_call(): pl.pallas_call(functools.partial(layer_kernel, nz, direct), out_shape=[ja...  143 us
    pallas_call x1, Pallas kernels, final_call(): pl.pallas_call(functools.partial(final_kernel, direct, shards), out_shape...  6.35 us

profile of v3, /device:TPU:0, one launch (start us, length us, event | category | flops | bytes accessed | tf_op | source)
XLA Modules:
  0.0 150.7 jit_solution(13320474812529308844)
XLA Ops:
  0.7 143.5 %layer.1 = (bf16[1024,768]{1,0:T(8,128)(2,1)}, bf16[768,768]{1,0:T(8,128)(2,1)}, bf16[1024,768]{1,0:T(8,128)(2,1)}, bf16[768,768]{1,0:T(8,128)(2,1)}, f32[16,768...) custom-call(s32[1,3]{1,0:T(1,128)} %lens.3, ...), custom_call_target="tpu_custom_call" | custom-call | flops 64000000000 | bytes 40000000 | tf_op jit(solution)/shard_map/layer/pallas_call | solution.py:673
  144.1 6.4 %final.1 = (bf16[1024,768]{1,0:T(8,128)(2,1)}, f32[1024,768]{1,0:T(8,128)}, f32[24,2304]{1,0:T(8,128)}, f32[24,768]{1,0:T(8,128)}, f32[24,3072]{1,0:T(8,128)}, /...) custom-call(s32[1,3]{1,0:T(1,128)} %lens.3, ...), custom_call_target="tpu_custom_call" | custom-call | flops 1000000 | bytes 12000000 | tf_op jit(solution)/shard_map/final/pallas_call | solution.py:749

commit v4 on v3

--- a/solution.py
+++ b/solution.py
@@ -146,6 +146,21 @@
     def place(u):
         return u if not direct else u % 5
 
+    def column(u, to, slot):
+        return remote(gs.at[c, home, u], r3s.at[slot], j_send.at[u], j_recv.at[slot], (b % 4 + 4 * to, c))
+
+    def column_send(u):
+        near = 2 - u // 2
+        pl.when(zz == u + 1 - 2 * (u % 2))(lambda: column(u, u, 0).start())
+        pl.when(zz == 3 - 3 * (u // 2))(lambda: column(u, near, 2 + u % 2).start())
+
+    def column_pass(u):
+        @pl.when(zz == 2 - u // 2)
+        def _():
+            column(u, u, 2 + u % 2).wait_recv()
+            add_into(gs.at[c, home, u], r3s.at[2 + u % 2])
+            column(u, u, 1).start()
+
     def copies(kind, u, stage):
         slot = u % 2
         if kind == "s":
@@ -156,8 +171,7 @@
                         for k in range(2)]
             if stage == 2:
                 return [remote(gs.at[c, give2, u], r2s.at[u % 4], s_send.at[u, 3], s_recv.at[u, 3], n2nd)]
-            return [remote(gs.at[c, home, z], r3s.at[i], j_send.at[i], j_recv.at[i], (b % 4 + 4 * z, c))
-                    for i, z in enumerate(zpeers)]
+            return [column(u, u, 0)]
         g = ge.at[place(u)]
         if stage == 0:
             return [remote(g.at[1 - c], r0e.at[slot], e_send.at[u, 0], e_recv.at[u, 0], partner)]
@@ -203,17 +217,23 @@
                     add_into(g.at[keep[k]], r1e.at[u % 4, k])
             elif stage == 3:
                 add_into(g.at[home], r2e.at[u % 4])
-        if kind == "e" or stage < 3:
+        if kind == "s" and stage == 3:
+            column_send(u)
+        else:
             start(kind, u, stage)
 
     def settle(kind, u):
-        finish(kind, u, 3)
         if kind == "s":
+            for n in range(nz):
+                pl.when(zz != n)(lambda n=n: copies("s", n, 3)[0].wait_send())
+            for i in range(2):
+                column(0, 0, i).wait_recv()
             total = gs[c, home, zz].astype(f32)
-            for i in range(nz - 1):
+            for i in range(2):
                 total = total + r3s[i].astype(f32)
             os_[...] = total
             return
+        finish(kind, u, 3)
         total = ge[place(u), c, home, zz].astype(f32)
         for i in range(nz - 1):
             total = total + r3e[u % 4, i].astype(f32)
@@ -236,8 +256,8 @@
             for kind, u, stage in todo:
                 if stage == 4:
                     settle(kind, u)
-                elif stage == "join":
-                    start(kind, u, 3)
+                elif stage == "pass":
+                    column_pass(u)
                 else:
                     advance(kind, u, stage)
 
@@ -413,6 +433,7 @@
                 dn[rows, :] += nt(de, we[:, cols])
                 bias_sum = bias_sum + jnp.sum(de.astype(f32), axis=0, keepdims=True)
                 if t == 0:
+                    steps([("s", j - 3, 3)], j >= 3)
                     steps([("s", j - 2, 2)], j >= 2)
                 elif t == 1:
                     steps([("s", j - 1, 1)], j >= 1)
@@ -481,7 +502,7 @@
                     dot[128 * h : 128 * h + 128, rows] = with_spare(
                         h % 2, dct[64 * h : 64 * h + 64, :], spare_rows(*split3(-inner)))
                 for n, todo in enumerate((
-                    [("s", 3, 1)], [("e", 3, 1)], [("e", 1, 2)], [("s", 2, 2)])):
+                    [("s", 2, 2), ("s", 3, 1), ("s", 0, "pass")], [("s", 1, 3), ("e", 3, 1)], [("e", 1, 2)], [("e", 0, 3)])):
                     if i == n:
                         steps(todo)
                 dpb = jnp.sum(ga.astype(f32), axis=0, keepdims=True)
@@ -547,15 +568,6 @@
                         dqt[half, qrows] = dq_part
                     else:
                         dqt[half, qrows] += dq_part
-                    if n == len(jobs) // 2:
-                        for r, todo in enumerate((
-                            [("s", 0, 3), ("e", 0, 3), ("s", 1, 3), ("e", 2, 2), ("e", 4, 1)],
-                            [("e", 0, 4), ("e", 1, 3), ("s", 3, 2), ("e", 3, 2)],
-                            [("s", 2, 3), ("e", 2, 3), ("e", 4, 2), ("e", 5, 1)],
-                            [("e", 1, 4), ("s", 3, 3), ("e", 3, 3)],
-                            [("e", 2, 4), ("s", 0, "join"), ("e", 4, 3), ("e", 5, 2), ("e", 6, 1)],
-                            [("e", 3, 4)])):
-                            steps(todo, p == r)
                     if s == 1 and qi == tiles - 1:
                         dqkv[krows, pl.ds(D + pat, 128)] = jnp.where(lane < 64, dk[0], dk[1]).astype(bf16)
                         dvp = jnp.where(lane < 64, dv[0], dv[1]).astype(bf16)
@@ -565,6 +577,14 @@
                 dqkv[:, pcols] = dq
                 vec[2:3, pcols] = jnp.sum(dq.astype(f32), axis=0, keepdims=True)
                 vec[3:4, pcols] = dv_sum
+                for r, todo in enumerate((
+                    [("s", 3, 2), ("s", 2, 3), ("e", 2, 2), ("e", 4, 1), ("s", 1, "pass")],
+                    [("e", 0, 4), ("s", 3, 3), ("e", 1, 3), ("e", 3, 2), ("s", 2, "pass")],
+                    [("e", 2, 3), ("e", 4, 2), ("e", 5, 1), ("s", 3, "pass")],
+                    [("e", 1, 4), ("e", 3, 3)],
+                    [("e", 2, 4), ("e", 4, 3), ("e", 5, 2), ("e", 6, 1)],
+                    [("e", 3, 4)])):
+                    steps(todo, p == r)
                 @pl.when(p % 2 == 1)
                 def _():
                     k = p // 2
@@ -576,6 +596,7 @@
                                 ge[at_ + (slice(None), slice(128 * w, 128 * w + 128))] = part
                     start("e", 5 + k, 0)
 
+                steps([("e", 6, 2)], p == PAIRS - 1)
                 return 0
 
             lax.fori_loop(0, PAIRS, pair, 0)
@@ -588,7 +609,7 @@
             back, dgain, dshift = norm_back(x[rows, :].astype(f32), gain1[...].reshape(1, D), g)
             m[rows, :] = (dn[rows, :] + back).astype(bf16)
             for n, todo in enumerate((
-                [("e", 4, 4), ("e", 5, 3), ("e", 6, 2), ("e", 7, 1)], [("s", 0, 4)], [], [("e", 7, 2)])):
+                [("e", 7, 1), ("e", 4, 4), ("e", 5, 3)], [("s", 0, 4)], [("e", 6, 3)], [("e", 7, 2)])):
                 steps(todo, i == n)
             return sums[0] + dgain, sums[1] + dshift
 
@@ -617,7 +638,7 @@
         ends.append(cp)
 
     if direct:
-        steps([("e", 5, 4), ("e", 6, 3), ("e", 7, 3)])
+        steps([("e", 5, 4), ("e", 7, 3)])
         total_hop(0)
         for cp in total_copies(1):
             cp.start()
@@ -663,11 +684,11 @@
             pltpu.VMEM((2, 4, 96, D), bf16), pltpu.VMEM((2, 4, nz) + unit, bf16),
             pltpu.VMEM((4, 2, 96, D), bf16), pltpu.VMEM((4, 2, nz) + unit, bf16),
             pltpu.VMEM((4, 96, D), bf16), pltpu.VMEM((4, nz) + unit, bf16),
-            pltpu.VMEM((nz - 1, 96, D), bf16), pltpu.VMEM((4, nz - 1) + unit, bf16),
+            pltpu.VMEM((4, 96, D), bf16), pltpu.VMEM((4, nz - 1) + unit, bf16),
             pltpu.VMEM((24, 3 * D), f32), pltpu.VMEM((24, D), f32), pltpu.VMEM((24, FF), f32), pltpu.VMEM((96, D), f32),
             pltpu.SemaphoreType.DMA((4, 4)), pltpu.SemaphoreType.DMA((4, 4)),
             pltpu.SemaphoreType.DMA((8, 7)), pltpu.SemaphoreType.DMA((8, 7)),
-            pltpu.SemaphoreType.DMA((3,)), pltpu.SemaphoreType.DMA((3,)),
+            pltpu.SemaphoreType.DMA((nz,)), pltpu.SemaphoreType.DMA((4,)),
             pltpu.SemaphoreType.DMA((10,)), pltpu.SemaphoreType.DMA((10,)),
         ]
     return pl.pallas_call(
@@ -707,24 +728,6 @@
     for group in loads:
         for cp in group:
             cp.start()
-    for src, dst in zip(grads, grads_to):
-        dst[...] = src[...]
-    if direct:
-        me = lax.axis_index("batch") * 2 + lax.axis_index("seq")
-
-        def columns(v, first, n):
-            shape = (D, 128)
-            pick = (row_ids(shape) == lane_ids(shape) + first) & (lane_ids(shape) < n)
-            return jnp.dot(v, pick.astype(f32), precision=lax.Precision.HIGHEST, preferred_element_type=f32)
-
-        n = D // shards
-        narrow = columns(vec[...], n * me, n)
-        for i in range(8):
-            parts[i][...] = narrow[i, :n]
-        n = FF // shards
-        wide = columns(vec[8:12, :], n * (me % (D // n)), n)
-        wide = jnp.sum(jnp.where(row_ids(wide.shape) == me // (D // n), wide, 0.0), axis=0)
-        parts[8][...] = wide[:n]
     saves = []
     for t in range(tiles):
         for cp in loads[t]:
@@ -739,6 +742,24 @@
         for i, (src, dst) in enumerate(((own, out), (res, ig))):
             saves.append(pltpu.make_async_copy(src.at[pl.ds(t * BLK, BLK)], dst.at[pl.ds(t * BLK, BLK)], save_sem.at[t, i]))
             saves[-1].start()
+    for src, dst in zip(grads, grads_to):
+        dst[...] = src[...]
+    if direct:
+        me = lax.axis_index("batch") * 2 + lax.axis_index("seq")
+
+        def columns(v, first, n):
+            shape = (D, 128)
+            pick = (row_ids(shape) == lane_ids(shape) + first) & (lane_ids(shape) < n)
+            return jnp.dot(v, pick.astype(f32), precision=lax.Precision.HIGHEST, preferred_element_type=f32)
+
+        n = D // shards
+        narrow = columns(vec[...], n * me, n)
+        for i in range(8):
+            parts[i][...] = narrow[i, :n]
+        n = FF // shards
+        wide = columns(vec[8:12, :], n * (me % (D // n)), n)
+        wide = jnp.sum(jnp.where(row_ids(wide.shape) == me // (D // n), wide, 0.0), axis=0)
+        parts[8][...] = wide[:n]
     for cp in saves:
         cp.wait()
 

time: 151 us -> 144 us (0.954)
  Pallas kernels: 150 us -> 143 us
    pallas_call x1, Pallas kernels: 143 us -> 136 us  [layer_call(): pl.pallas_call(functools.partial(layer_kernel, nz, direct), out_shape=[ja...]
where the time goes in v4:
time: 144 us
  Pallas kernels  143 us (99%)
    pallas_call x1, Pallas kernels, layer_call(): pl.pallas_call(functools.partial(layer_kernel, nz, direct), out_shape=[ja...  136 us
    pallas_call x1, Pallas kernels, final_call(): pl.pallas_call(functools.partial(final_kernel, direct, shards), out_shape...  6.76 us

profile of v4, /device:TPU:0, one launch (start us, length us, event | category | flops | bytes accessed | tf_op | source)
XLA Modules:
  0.0 143.7 jit_solution(10801433198374007778)
XLA Ops:
  0.7 136.2 %layer.1 = (bf16[1024,768]{1,0:T(8,128)(2,1)}, bf16[768,768]{1,0:T(8,128)(2,1)}, bf16[1024,768]{1,0:T(8,128)(2,1)}, bf16[768,768]{1,0:T(8,128)(2,1)}, f32[16,768...) custom-call(s32[1,3]{1,0:T(1,128)} %lens.3, ...), custom_call_target="tpu_custom_call" | custom-call | flops 64000000000 | bytes 40000000 | tf_op jit(solution)/shard_map/layer/pallas_call | solution.py:694
  136.8 6.8 %final.1 = (bf16[1024,768]{1,0:T(8,128)(2,1)}, f32[1024,768]{1,0:T(8,128)}, f32[24,2304]{1,0:T(8,128)}, f32[24,768]{1,0:T(8,128)}, f32[24,3072]{1,0:T(8,128)}, /...) custom-call(s32[1,3]{1,0:T(1,128)} %lens.3, ...), custom_call_target="tpu_custom_call" | custom-call | flops 1000000 | bytes 12000000 | tf_op jit(solution)/shard_map/final/pallas_call | solution.py:770
